TPU v7x, 32 devices: a whole 2x2x4 slice. The times are simulated.
32 devices in a mesh: leaf: 8 (over z, x), rhs: 4 (over y, core).
Axes of the slice: x: 2, y: 2, z: 4, core: 2. Of those that a mesh axis runs over, the one named last changes fastest.
Arguments:
- rhs_vectors: bfloat16 [32, 16384], P('rhs', 'leaf'), may hold values from -6 to 6
- diag_inverse: bfloat16 [16384, 2048], P('leaf'), may hold values from -1 to 2
- left_factors: bfloat16 [16384, 192], P('leaf'), may hold values from -0.375 to 0.375
- right_factors: bfloat16 [16384, 192], P('leaf'), may hold values from -0.125 to 0.125
- ranks: int32 [3], replicated, may hold values from 32 to 64, as said below
Outputs:
- solution: float32 [32, 16384], P('rhs', 'leaf')
Inputs may be any that keep to these rules, and one draw needn't show every extreme that they name: `ranks`: some level has rank exactly 64.
All inputs are finite; a program needn't handle non-finite values.
Results may differ from a plain program's by a relative error of at most 0.0031.
Values sent between devices are 32-bit elements; how exact they have to be, the bound alone decides.
A program may use at most 64 MiB of HBM per device.

v0:
```python
import jax
import jax.numpy as jnp
from jax import lax
from jax.sharding import PartitionSpec as P

best_precision = lax.Precision.HIGHEST


def swapped(x, axis, distance):
    return lax.ppermute(x, axis, [(i, i ^ 1 << distance) for i in range(lax.axis_size(axis))])


def compose(former, latter):
    joined_map = jnp.dot(latter[0], former[0], precision=best_precision)
    joined_shift = jnp.dot(latter[0], former[1], precision=best_precision) + latter[1]
    return (joined_map, joined_shift)


def on_device(rhs_vectors, diag_inverse, left_factors, right_factors, ranks):
    leaves = lax.axis_size("leaf")
    levels = leaves.bit_length() - 1
    state_rows = left_factors.shape[1]
    rank_top = state_rows // levels
    position = lax.axis_index("leaf")
    row_level = jnp.arange(state_rows, dtype=jnp.int32) // rank_top
    row_rank = jnp.arange(state_rows, dtype=jnp.int32) % rank_top
    level_table = jnp.arange(levels, dtype=jnp.int32)
    rank_of = jnp.sum(
        jnp.where(row_level[:, None] == level_table[None, :], ranks[None, :], 0), axis=1
    )
    column_keep = (row_rank < rank_of).astype(jnp.bfloat16)
    left_kept = left_factors * column_keep[None, :]
    right_kept = right_factors * column_keep[None, :]
    right_wide = right_kept.astype(jnp.float32)
    level_bit = (position >> row_level & 1).astype(jnp.float32)
    span_mask = jnp.left_shift(jnp.int32(2), row_level)
    reset_keep = jnp.where((position + 1) % span_mask == 0, 0.0, 1.0).astype(jnp.float32)
    mapped = jnp.dot(diag_inverse, left_kept, preferred_element_type=jnp.float32).astype(
        jnp.bfloat16
    )
    coupling = jnp.einsum("mr,ms->rs", right_kept, mapped, preferred_element_type=jnp.float32)
    identity = jnp.eye(state_rows, dtype=jnp.float32)
    open_rows = 1.0 - level_bit
    step_map = reset_keep[:, None] * (identity - open_rows[:, None] * coupling * level_bit[None, :])
    inverse_rhs = jnp.einsum(
        "km,nm->kn", rhs_vectors, diag_inverse, preferred_element_type=jnp.float32
    )
    projected = jnp.einsum("mr,km->rk", right_wide, inverse_rhs, precision=best_precision)
    step_shift = (reset_keep * open_rows)[:, None] * projected
    empty_shift = jnp.zeros_like(step_shift)
    total_map, total_shift = (step_map, step_shift)
    prefix_map, prefix_shift = (identity, empty_shift)
    for bit_level in range(levels):
        lowest = bit_level * rank_top
        got_map, got_shift = swapped((total_map[lowest:], total_shift[lowest:]), "leaf", bit_level)
        partner_map = jnp.concatenate(
            [jnp.zeros((lowest, state_rows), jnp.float32), got_map], axis=0
        )
        partner_shift = jnp.concatenate(
            [jnp.zeros((lowest, step_shift.shape[1]), jnp.float32), got_shift], axis=0
        )
        upper_half = position >> bit_level & 1 == 1
        after_map, after_shift = compose((partner_map, partner_shift), (total_map, total_shift))
        before_map, before_shift = compose((total_map, total_shift), (partner_map, partner_shift))
        joined_map, joined_shift = compose((partner_map, partner_shift), (prefix_map, prefix_shift))
        total_map = jnp.where(upper_half, after_map, before_map)
        total_shift = jnp.where(upper_half, after_shift, before_shift)
        prefix_map = jnp.where(upper_half, joined_map, prefix_map)
        prefix_shift = jnp.where(upper_half, joined_shift, prefix_shift)
    correction = jnp.einsum(
        "ms,sk->km",
        mapped.astype(jnp.float32),
        level_bit[:, None] * prefix_shift,
        precision=best_precision,
    )
    return inverse_rhs - correction


def solution(mesh):
    in_specs = (P("rhs", "leaf"), P("leaf", None), P("leaf", None), P("leaf", None), P())
    out_specs = P("rhs", "leaf")
    return jax.shard_map(
        on_device, mesh=mesh, in_specs=in_specs, out_specs=out_specs, check_vma=False
    )
```

profile of v0, /device:TPU:0, one launch (start us, length us, event | category | flops | bytes accessed | tf_op | source)
XLA Modules:
  0.0 35.7 jit_solution(7561167670166274802)
XLA Ops:
  0.0 0.0 copy-start
  0.0 0.0 copy-start.2
  0.0 0.8 %select_reduce_fusion = s32[192]{0:T(256)S(1)} fusion(s32[3]{0:T(128)} %param.9, s32[192]{0:T(256)S(1)} %and_select_fusion.2), kind=kLoop, calls=%fused_computation.36 | loop fusion | flops 1536 | bytes 1548 | tf_op jit(solution)/shard_map/reduce_sum | solution.py:28
  0.8 0.0 copy-start.1
  0.8 0.1 fusion.23
  1.0 0.0 copy-done
  1.0 5.8 %fusion.29 = f32[8,2048]{1,0:T(8,128)S(1)} fusion(bf16[8,2048]{1,0:T(8,128)(2,1)S(1)} %copy-done, bf16[2048,2048]{1,0:T(8,128)(2,1)} %param.6), kind=kOutput, calls=%fused_computation.58 | convolution fusion | flops 67108864 | bytes 8486912 | tf_op jit(solution)/shard_map/km,nm->kn/dot_general | solution.py:45
  6.8 0.0 copy-done.2
  6.8 0.8 %convolution_multiply_fusion.1 = f32[192,8]{0,1:T(8,128)S(1)} fusion(f32[8,2048]{1,0:T(8,128)S(1)} %fusion.29, bf16[2048,192]{0,1:T(8,128)(2,1)S(1)} %copy-done.2, bf16[192]{0:T(256)(128)(2,1)S(1)} %compare_convert_fusion, f32[192]{0:T(256)S(1)} %fusion.23), kind=kOutput, calls=%fused_computation.18 | convolution fusion | flops 38143488 | bytes 859264 | tf_op jit(solution)/shard_map/mr,km->rk/dot_general | solution.py:48
  7.6 3.0 %collective-permute-start.2 = (f32[192,8]{0,1:T(8,128)S(1)}, f32[192,8]{0,1:T(8,128)S(1)}, u32[]{:S(2)}, u32[]{:S(2)}) collective-permute-start(f32[192,8]{0,1:T(8,128)S(1)} %convolution_multiply_fusion.1), channel_id=1, source_target_pairs={{0,4},{4,0},{8,12},{12,8},{16,20},{20,16},{24,28},{28,24},{1,5},{5... | collective-permute-start | bytes 18440 | tf_op jit(solution)/shard_map/ppermute | solution.py:10
  10.5 0.1 compare_select_fusion.1
  10.7 0.0 copy-done.1
  10.7 4.1 %convolution_convert_fusion = bf16[192,2048]{1,0:T(8,128)(2,1)S(1)} fusion(bf16[2048,2048]{1,0:T(8,128)(2,1)S(1)} %copy-done.1, bf16[2048,192]{0,1:T(8,128)(2,1)} %param.7, bf16[192]{0:T(256)(128)(2,1)S(1)} %compare_convert_fusion), kind=kOutput, calls=%fused_computation | convolution fusion | flops 1611399168 | bytes 9961856 | tf_op jit(solution)/shard_map/dot_general | solution.py:38
  14.8 0.4 %fusion.2 = f32[192,192]{1,0:T(8,128)S(1)} fusion(bf16[192,2048]{1,0:T(8,128)(2,1)S(1)} %convolution_convert_fusion, bf16[2048,192]{0,1:T(8,128)(2,1)S(1)} %copy-done.2, bf16[192]{0:T(256)(128)(2,1)S(1)} %compare_convert_fusion, f32[192]{0:T(256)S(1)} %and_convert_fusion, f32[192]{0:T(256)S(1)} %get-tuple-element.6, f32[192]{0:T(256)S(1)} %get-tuple-element.5), kind=kOutput, calls=%fused_computation.8 | convolution fusion | flops 151609344 | bytes 1723008 | tf_op jit(solution)/shard_map/mr,ms->rs/dot_general | solution.py:41
  15.2 0.1 collective-permute-start
  15.3 0.0 collective-permute-done.2
  15.3 0.1 convolution_select_fusion.3
  15.4 6.2 %collective-permute-done = f32[192,192]{1,0:T(8,128)S(1)} collective-permute-done((f32[192,192]{1,0:T(8,128)S(1)}, f32[192,192]{1,0:T(8,128)S(1)}, u32[]{:S(2)}, u32[]{:S(2)}) %collective-permute-start) | collective-permute-done | bytes 147488 | tf_op jit(solution)/shard_map/ppermute | solution.py:10
  21.6 0.2 convolution_add_fusion.2
  21.8 0.3 fusion.6
  22.1 0.1 slice.13
  22.3 1.6 %collective-permute-start.3 = (f32[128,8]{0,1:T(8,128)S(1)}, f32[128,8]{0,1:T(8,128)S(1)}, u32[]{:S(2)}, u32[]{:S(2)}) collective-permute-start(f32[128,8]{0,1:T(8,128)S(1)} %slice.13), channel_id=1, source_target_pairs={{0,8},{4,12},{8,0},{12,4},{16,24},{20,28},{24,16},{28,20},{1,9},{5... | collective-permute-start | bytes 12296 | tf_op jit(solution)/shard_map/ppermute | solution.py:10
  23.8 0.3 fusion.30
  24.2 0.3 convolution_select_fusion.1
  24.5 0.5 %collective-permute-start.1 = (f32[128,192]{1,0:T(8,128)S(1)}, f32[128,192]{1,0:T(8,128)S(1)}, u32[]{:S(2)}, u32[]{:S(2)}) collective-permute-start(f32[128,192]{1,0:T(8,128)S(1)} %slice.12), channel_id=1, source_target_pairs={{0,8},{4,12},{8,0},{12,4},{16,24},{20,28},{24,16},{28,20},{1,9},{5... | collective-permute-start | bytes 294920 | tf_op jit(solution)/shard_map/ppermute | solution.py:10
  25.0 0.3 convolution_select_fusion.2
  25.3 0.6 %collective-permute-done.3 = f32[128,8]{0,1:T(8,128)S(1)} collective-permute-done((f32[128,8]{0,1:T(8,128)S(1)}, f32[128,8]{0,1:T(8,128)S(1)}, u32[]{:S(2)}, u32[]{:S(2)}) %collective-permute-start.3) | collective-permute-done | bytes 4128 | tf_op jit(solution)/shard_map/ppermute | solution.py:10
  25.9 0.2 fusion.3
  26.1 0.3 fusion.17
  26.4 3.1 %collective-permute-done.1 = f32[128,192]{1,0:T(8,128)S(1)} collective-permute-done((f32[128,192]{1,0:T(8,128)S(1)}, f32[128,192]{1,0:T(8,128)S(1)}, u32[]{:S(2)}, u32[]{:S(2)}) %collective-permute-start.1) | collective-permute-done | bytes 98336 | tf_op jit(solution)/shard_map/ppermute | solution.py:10
  29.6 0.2 fusion.13
  29.8 0.1 fusion.20
  29.9 2.6 %collective-permute-start.4 = (f32[64,8]{0,1:T(8,128)S(1)}, f32[64,8]{0,1:T(8,128)S(1)}, u32[]{:S(2)}, u32[]{:S(2)}) collective-permute-start(f32[64,8]{0,1:T(8,128)S(1)} %fusion.20), channel_id=1, source_target_pairs={{0,16},{4,20},{8,24},{12,28},{16,0},{20,4},{24,8},{28,12},{1,17},{... | collective-permute-start | bytes 6152 | tf_op jit(solution)/shard_map/ppermute | solution.py:10
  32.5 0.3 convolution_select_fusion
  32.9 1.5 %collective-permute-done.4 = f32[64,8]{0,1:T(8,128)S(1)} collective-permute-done((f32[64,8]{0,1:T(8,128)S(1)}, f32[64,8]{0,1:T(8,128)S(1)}, u32[]{:S(2)}, u32[]{:S(2)}) %collective-permute-start.4) | collective-permute-done | bytes 2080 | tf_op jit(solution)/shard_map/ppermute | solution.py:10
  34.4 0.2 fusion.5
  34.6 1.1 %convolution_subtract_fusion = f32[8,2048]{1,0:T(8,128)} fusion(f32[8,2048]{1,0:T(8,128)S(1)} %fusion.29, f32[192,8]{0,1:T(8,128)S(1)} %fusion.5, bf16[192,2048]{1,0:T(8,128)(2,1)S(1)} %convolution_convert_fusion), kind=kOutput, calls=%fused_computation.1 | convolution fusion | flops 37765120 | bytes 923648 | tf_op jit(solution)/shard_map/ms,sk->km/dot_general | solution.py:70
  (4 shorter events, 0.0 us)
Async XLA Ops:
  0.0 1.0 %copy-start = (bf16[8,2048]{1,0:T(8,128)(2,1)S(1)}, bf16[8,2048]{1,0:T(8,128)(2,1)}, u32[]{:S(2)}) copy-start(bf16[8,2048]{1,0:T(8,128)(2,1)} %param.5) | copy-start | bytes 98308
  0.0 6.8 %copy-start.2 = (bf16[2048,192]{0,1:T(8,128)(2,1)S(1)}, bf16[2048,192]{0,1:T(8,128)(2,1)}, u32[]{:S(2)}) copy-start(bf16[2048,192]{0,1:T(8,128)(2,1)} %param.8) | copy-start | bytes 2359300
  0.8 9.9 %copy-start.1 = (bf16[2048,2048]{1,0:T(8,128)(2,1)S(1)}, bf16[2048,2048]{1,0:T(8,128)(2,1)}, u32[]{:S(2)}) copy-start(bf16[2048,2048]{1,0:T(8,128)(2,1)} %param.6) | copy-start | bytes 25165828
  7.6 7.7 %collective-permute-start.2 = (f32[192,8]{0,1:T(8,128)S(1)}, f32[192,8]{0,1:T(8,128)S(1)}, u32[]{:S(2)}, u32[]{:S(2)}) collective-permute-start(f32[192,8]{0,1:T(8,128)S(1)} %convolution_multiply_fusion.1), channel_id=1, source_target_pairs={{0,4},{4,0},{8,12},{12,8},{16,20},{20,16},{24,28},{28,24},{1,5},{5... | collective-permute-start | bytes 18440 | tf_op jit(solution)/shard_map/ppermute | solution.py:10
  15.2 6.4 %collective-permute-start = (f32[192,192]{1,0:T(8,128)S(1)}, f32[192,192]{1,0:T(8,128)S(1)}, u32[]{:S(2)}, u32[]{:S(2)}) collective-permute-start(f32[192,192]{1,0:T(8,128)S(1)} %fusion.2), channel_id=1, source_target_pairs={{0,4},{4,0},{8,12},{12,8},{16,20},{20,16},{24,28},{28,24},{1,5},{5... | collective-permute-start | bytes 442376 | tf_op jit(solution)/shard_map/ppermute | solution.py:10
  22.3 3.7 %collective-permute-start.3 = (f32[128,8]{0,1:T(8,128)S(1)}, f32[128,8]{0,1:T(8,128)S(1)}, u32[]{:S(2)}, u32[]{:S(2)}) collective-permute-start(f32[128,8]{0,1:T(8,128)S(1)} %slice.13), channel_id=1, source_target_pairs={{0,8},{4,12},{8,0},{12,4},{16,24},{20,28},{24,16},{28,20},{1,9},{5... | collective-permute-start | bytes 12296 | tf_op jit(solution)/shard_map/ppermute | solution.py:10
  24.5 5.0 %collective-permute-start.1 = (f32[128,192]{1,0:T(8,128)S(1)}, f32[128,192]{1,0:T(8,128)S(1)}, u32[]{:S(2)}, u32[]{:S(2)}) collective-permute-start(f32[128,192]{1,0:T(8,128)S(1)} %slice.12), channel_id=1, source_target_pairs={{0,8},{4,12},{8,0},{12,4},{16,24},{20,28},{24,16},{28,20},{1,9},{5... | collective-permute-start | bytes 294920 | tf_op jit(solution)/shard_map/ppermute | solution.py:10
  29.9 4.5 %collective-permute-start.4 = (f32[64,8]{0,1:T(8,128)S(1)}, f32[64,8]{0,1:T(8,128)S(1)}, u32[]{:S(2)}, u32[]{:S(2)}) collective-permute-start(f32[64,8]{0,1:T(8,128)S(1)} %fusion.20), channel_id=1, source_target_pairs={{0,16},{4,20},{8,24},{12,28},{16,0},{20,4},{24,8},{28,12},{1,17},{... | collective-permute-start | bytes 6152 | tf_op jit(solution)/shard_map/ppermute | solution.py:10
where the time goes:
time: 35.9 us; the launch traced here: 35.7 us
  matrix products  15 us (42%)
  waiting for transfers between devices  11.5 us (32%)
  starting transfers between devices  7.8 us (22%)
  other arithmetic  1.22 us (3%)
    ppermute x5, waiting for transfers between devices, swapped(): lax.ppermute(x, axis, [(i, i ^ 1 << distance) for i in range(lax.axis_siz...  11.5 us
    ppermute x5, starting transfers between devices, swapped(): lax.ppermute(x, axis, [(i, i ^ 1 << distance) for i in range(lax.axis_siz...  7.8 us
    dot_general x1, matrix products, on_device(): jnp.einsum('km,nm->kn', rhs_vectors, diag_inverse, preferred_element_type...  5.79 us
    dot_general x1, matrix products, on_device(): jnp.dot(diag_inverse, left_kept, preferred_element_type=jnp.float32)  4.07 us
    dot_general x7, matrix products, compose(): jnp.dot(latter[0], former[1], precision=best_precision) + latter[1]  1.58 us
    dot_general x4, matrix products, compose(): joined_map = jnp.dot(latter[0], former[0], precision=best_precision)  1.21 us
    dot_general x1, matrix products, on_device(): jnp.einsum('ms,sk->km', mapped.astype(jnp.float32), level_bit[:, None] *...  1.12 us
    reduce_sum x1, other arithmetic, on_device(): jnp.sum(jnp.where(row_level[:, None] == level_table[None, :], ranks[None,...  0.81 us
  transfers between devices with their start and end apart: 5, of which 4 were waited for; matrix products, arithmetic and copies ran while one was open for 18% of the time, Pallas kernels for 0%

commit v1 on v0

v1 whole, which is shorter than its diff:
```python
import functools

import jax
import jax.numpy as jnp
from jax import lax
from jax.experimental import pallas as pl
from jax.experimental.pallas import tpu as pltpu
from jax.sharding import PartitionSpec as P

LANES = 128
F32 = jnp.float32
BF16 = jnp.bfloat16


def split(x):
    high = x.astype(BF16)
    return high, (x - high.astype(F32)).astype(BF16)


def dot(a, b):
    return jnp.dot(a, b, preferred_element_type=F32)


def dot_split(a, b):
    a_high, a_low = split(a)
    b_high, b_low = split(b)
    return dot(a_high, b_high) + (dot(a_high, b_low) + dot(a_low, b_high))


def kernel(
    levels, rank_top, chunk,
    ranks_ref, b_ref, d_hbm, u_hbm, v_hbm, y_ref,
    d_buf, u_buf, v_buf, x_ref, acc_ref, wt_ref, c_ref, r_ref, total, got,
    d_sem, u_sem, v_sem, send_sem, got_sem,
):
    me = lax.axis_index("leaf")
    rows = d_buf.shape[0]
    chunks = rows // chunk
    state = u_buf.shape[1]
    count = b_ref.shape[0]
    tiles = total.shape[0]
    bits = [lax.rem(lax.div(me, 1 << l), 2) for l in range(levels)]

    def d_copy(m):
        at = pl.ds(pl.multiple_of(m * chunk, chunk), chunk)
        return pltpu.make_async_copy(d_hbm.at[at, :], d_buf.at[at, :], d_sem.at[m])

    u_copy = pltpu.make_async_copy(u_hbm, u_buf, u_sem)
    v_copy = pltpu.make_async_copy(v_hbm, v_buf, v_sem)
    u_copy.start()
    d_copy(0).start()
    v_copy.start()
    for m in range(1, chunks):
        d_copy(m).start()

    def sender_of(l):
        span = 2 << l
        return lax.div(me, span) * span + ((1 << l) - 1)

    def is_last(l):
        return lax.rem(me, 1 << l) == (1 << l) - 1

    got[...] = jnp.zeros_like(got)
    total[...] = jnp.zeros_like(total)
    barrier = pltpu.get_barrier_semaphore()
    for l in range(levels):
        @pl.when(bits[l] == 1)
        def _():
            pl.semaphore_signal(
                barrier, inc=1, device_id={"leaf": sender_of(l)},
                device_id_type=pl.DeviceIdType.MESH,
            )

    edge = state // LANES * LANES
    above = state - edge
    b = b_ref[...].astype(F32)
    pieces = [b, jnp.zeros((LANES - above - count, rows), F32)]
    if above:
        pieces = [jnp.zeros((above, rows), F32)] + pieces
    x_ref[:, edge:edge + LANES] = jnp.concatenate(pieces, axis=0).T.astype(BF16)
    u_copy.wait()
    if edge:
        x_ref[:, 0:edge] = u_buf[:, 0:edge]
    if above:
        x_ref[:, edge:state] = u_buf[:, edge:state]
    r_ref[...] = jnp.zeros_like(r_ref)

    def multiply(m):
        at = pl.ds(pl.multiple_of(m * chunk, chunk), chunk)
        return dot(d_buf[at, :], x_ref[...])

    def project(m, block):
        at = pl.ds(pl.multiple_of(m * chunk, chunk), chunk)
        turned = block.T
        w = turned[0:state].astype(BF16)
        c = turned[state:state + count]
        c_ref[:, at] = c
        high = c.astype(BF16).astype(F32)
        both = jnp.concatenate([high, c - high], axis=0).astype(BF16)
        wt_ref[:, at] = w
        v = v_buf[at, :]
        r_ref[0:state, :] += dot(w, v)
        r_ref[state:state + 2 * count, :] += dot(both, v)

    d_copy(0).wait()
    acc_ref[0] = multiply(0)
    v_copy.wait()

    def body(m, carry):
        d_copy(m).wait()
        before = acc_ref[lax.rem(m + 1, 2)]
        block = multiply(m)
        project(m - 1, before)
        acc_ref[lax.rem(m, 2)] = block
        return carry

    lax.fori_loop(1, chunks, body, 0)
    project(chunks - 1, acc_ref[(chunks - 1) % 2])

    lane = lax.broadcasted_iota(jnp.int32, (1, state), 1)
    limit = jnp.zeros((1, state), jnp.int32)
    for l in range(levels):
        limit = jnp.where(lane // rank_top == l, ranks_ref[l], limit)
    r = jnp.where(lane % rank_top < limit, r_ref[...], 0.0)
    for t in range(tiles):
        wide = min(LANES, state - t * LANES)
        part = r[:, t * LANES:t * LANES + wide]
        total[t, 0:count, 0:wide] = (
            part[state:state + count] + part[state + count:state + 2 * count]
        )
        total[t, count:count + state, 0:wide] = -part[0:state]

    def tile_of(l):
        return l * rank_top // LANES

    def tile_used(l, t):
        used = bits[0] < 0
        for c in range(l + 1, levels):
            if tile_of(c) == t:
                used = jnp.logical_or(used, bits[c] == 0)
        return used

    def row_block(m):
        if m is None:
            return pl.ds(0, count)
        return pl.ds(count + m * rank_top, rank_top)

    def copies(l):
        out = []
        last = (1 << l) - 1
        first = lax.div(me, 2 << l) * (2 << l) + (1 << l)
        for place in range(last, -1, -1):
            for m in [None] + list(range(l + 1, levels)):
                for t in range(tiles):
                    if t != tile_of(l) and (place != last or all(tile_of(c) != t for c in range(l + 1, levels))):
                        continue
                    condition = []
                    if m is not None:
                        condition.append(bits[m] == 1)
                    if t != tile_of(l):
                        condition.append(tile_used(l, t))
                    slot = 0 if m is None else m + 1
                    out.append((place, condition, pltpu.make_async_remote_copy(
                        src_ref=total.at[t, row_block(m), :],
                        dst_ref=got.at[l, t, row_block(m), :],
                        send_sem=send_sem.at[len(out)],
                        recv_sem=got_sem.at[l, t, slot],
                        device_id={"leaf": first + place},
                        device_id_type=pl.DeviceIdType.MESH,
                    )))
        return out

    def guarded(conditions, action):
        if conditions:
            pl.when(functools.reduce(jnp.logical_and, conditions))(action)
        else:
            action()

    def receive(l):
        for place, condition, copy in copies(l):
            if place != (1 << l) - 1:
                continue
            guarded(condition, copy.wait_recv)

    def receive_narrow(l):
        t = tile_of(l)
        for m in [None] + list(range(l + 1, levels)):
            copy = pltpu.make_async_remote_copy(
                src_ref=total.at[t, row_block(m), :],
                dst_ref=got.at[l, t, row_block(m), :],
                send_sem=send_sem.at[0],
                recv_sem=got_sem.at[l, t, 0 if m is None else m + 1],
                device_id={"leaf": sender_of(l)},
                device_id_type=pl.DeviceIdType.MESH,
            )
            guarded([] if m is None else [bits[m] == 1], copy.wait_recv)

    def join(l):
        own = tile_of(l)
        start = l * rank_top - own * LANES
        row = lax.broadcasted_iota(jnp.int32, (LANES, LANES), 0)
        inside = jnp.logical_and(row >= start, row < start + rank_top)

        def update(lo, hi):
            factor = got[l, own, lo:hi, :]
            for t in range(tiles):
                if all(tile_of(c) != t for c in range(l + 1, levels)):
                    continue
                at = count + own * LANES
                step = jnp.where(inside, total[t, at:at + LANES, :], 0.0)
                total[t, lo:hi, :] = (
                    total[t, lo:hi, :] + got[l, t, lo:hi, :] + dot_split(factor, step)
                )

        update(0, count)
        if l + 1 < levels:
            @pl.when(lax.div(me, 2 << l) > 0)
            def _():
                update(count + (l + 1) * rank_top, count + state)

    for l in range(levels):
        sends = jnp.logical_and(is_last(l), bits[l] == 0)
        if l:
            takes = jnp.logical_and(is_last(l), bits[l] == 1)
            others = jnp.logical_and(jnp.logical_not(is_last(l)), bits[l] == 1)
        else:
            takes, others = bits[l] == 1, None

        @pl.when(sends)
        def _():
            pl.semaphore_wait(barrier, 1 << l)
            for _, condition, copy in copies(l):
                guarded(condition, copy.start)

        @pl.when(takes)
        def _():
            receive(l)
            if l + 1 < levels:
                join(l)

        if others is not None:
            @pl.when(others)
            def _():
                receive_narrow(l)

    wide = tiles * LANES
    lane = lax.broadcasted_iota(jnp.int32, (1, LANES), 1)
    parts = [jnp.zeros((count, LANES), F32)] * tiles
    for l in range(levels - 1, -1, -1):
        t = tile_of(l)
        value = got[l, t, 0:count, :]
        if l + 1 < levels:
            value = value + dot_split(
                jnp.concatenate(parts, axis=1), got[l, t, count:count + wide, :]
            )
        start = l * rank_top - t * LANES
        inside = jnp.logical_and(lane >= start, lane < start + rank_top)
        parts[t] = jnp.where(inside, value, parts[t])
    p = jnp.concatenate(parts, axis=1)[:, 0:state]
    high = p.astype(BF16).astype(F32)
    both = jnp.concatenate([high, p - high], axis=0).astype(BF16)
    moved = dot(both, wt_ref[...])
    y_ref[...] = c_ref[...] - (moved[0:count] + moved[count:2 * count])

    for l in range(levels):
        @pl.when(jnp.logical_and(is_last(l), bits[l] == 0))
        def _():
            for _, condition, copy in copies(l):
                guarded(condition, copy.wait_send)


def on_device(rhs_vectors, diag_inverse, left_factors, right_factors, ranks):
    leaves = lax.axis_size("leaf")
    levels = leaves.bit_length() - 1
    count, rows = rhs_vectors.shape
    state = left_factors.shape[1]
    rank_top = state // levels
    tiles = pl.cdiv(state, LANES)
    wide = pl.cdiv(state + count, LANES) * LANES
    chunk = rows // 8
    most = 0
    for l in range(levels):
        most = max(most, ((1 << l) - 1 + tiles) * (levels - l))
    vmem = pl.BlockSpec(memory_space=pltpu.VMEM)
    hbm = pl.BlockSpec(memory_space=pl.ANY)
    return pl.pallas_call(
        functools.partial(kernel, levels, rank_top, chunk),
        out_shape=jax.ShapeDtypeStruct((count, rows), F32),
        in_specs=[pl.BlockSpec(memory_space=pltpu.SMEM), vmem, hbm, hbm, hbm],
        out_specs=vmem,
        scratch_shapes=[
            pltpu.VMEM(diag_inverse.shape, BF16),
            pltpu.VMEM((rows, state), BF16),
            pltpu.VMEM((rows, state), BF16),
            pltpu.VMEM((rows, wide), BF16),
            pltpu.VMEM((2, chunk, wide), F32),
            pltpu.VMEM((state, rows), BF16),
            pltpu.VMEM((count, rows), F32),
            pltpu.VMEM((state + 2 * count, state), F32),
            pltpu.VMEM((tiles, count + tiles * LANES, LANES), F32),
            pltpu.VMEM((levels, tiles, count + tiles * LANES, LANES), F32),
            pltpu.SemaphoreType.DMA((rows // chunk,)),
            pltpu.SemaphoreType.DMA,
            pltpu.SemaphoreType.DMA,
            pltpu.SemaphoreType.DMA((most,)),
            pltpu.SemaphoreType.DMA((levels, tiles, levels + 1)),
        ],
        compiler_params=pltpu.CompilerParams(
            collective_id=0, has_side_effects=True, vmem_limit_bytes=56 * 1024 * 1024
        ),
        cost_estimate=pl.CostEstimate(
            flops=2 * rows * rows * wide, bytes_accessed=2 * rows * (rows + 2 * state), transcendentals=0
        ),
    )(ranks, rhs_vectors, diag_inverse, left_factors, right_factors)


def solution(mesh):
    in_specs = (P("rhs", "leaf"), P("leaf", None), P("leaf", None), P("leaf", None), P())
    return jax.shard_map(
        on_device, mesh=mesh, in_specs=in_specs, out_specs=P("rhs", "leaf"), check_vma=False
    )
```

time: 35.9 us -> 23.7 us (0.66)
  the two profiles are of different devices: /device:TPU:0 before, /device:TPU:20 now
where the time goes in v1:
time: 23.7 us; the launch traced here: 23.4 us
  Pallas kernels  17.5 us (74%)
  local copies, waits for them, and re-layouts  5.94 us (25%)
    pallas_call x1, Pallas kernels, on_device(): pl.pallas_call(functools.partial(kernel, levels, rank_top, chunk), out_sh...  17.5 us
    unnamed x3, local copies, waits for them, and re-layouts  5.94 us

profile of v1, /device:TPU:20, one launch (start us, length us, event | category | flops | bytes accessed | tf_op | source)
XLA Modules:
  0.0 23.4 jit_solution(2999528364977830203)
XLA Ops:
  0.0 2.2 %copy.6.u_hbm = bf16[2048,192]{1,0:T(8,128)(2,1)} copy(bf16[2048,192]{0,1:T(8,128)(2,1)} %param.7) | data formatting | bytes 1572864 | tf_op args[2]
  2.2 2.2 %copy.7.v_hbm = bf16[2048,192]{1,0:T(8,128)(2,1)} copy(bf16[2048,192]{0,1:T(8,128)(2,1)} %param.8) | data formatting | bytes 1572864 | tf_op args[3]
  4.5 17.5 %shard_map.55 = f32[8,2048]{1,0:T(8,128)} custom-call(s32[3]{0:T(128)} %ranks_ref.1, bf16[8,2048]{1,0:T(8,128)(2,1)} %b_ref.1, bf16[2048,2048]{1,0:T(8,128)(2,1)} %d_hbm.1, bf16[2048,192]{1,0:T(8,128)(2,1)} %copy.6.u_hbm, bf16[2048,192]{1,0:T(8,128)(2,1)} %copy.7.v_hbm), custom_call_target="tpu_custom_call" | custom-call | flops 2147483648 | bytes 9961472 | tf_op jit(solution)/shard_map/pallas_call | solution.py:286
  21.9 1.5 %copy.9 = f32[8,2048]{1,0:T(8,128)} copy(f32[8,2048]{1,0:T(8,128)} %shard_map.55) | data formatting | bytes 131072

commit v2 on v1

--- a/solution.py
+++ b/solution.py
@@ -21,6 +21,10 @@
     return jnp.dot(a, b, preferred_element_type=F32)
 
 
+def dot_turned(a, b):
+    return lax.dot_general(a, b, (((1,), (1,)), ((), ())), preferred_element_type=F32)
+
+
 def dot_split(a, b):
     a_high, a_low = split(a)
     b_high, b_low = split(b)
@@ -29,14 +33,14 @@
 
 def kernel(
     levels, rank_top, chunk,
-    ranks_ref, b_ref, d_hbm, u_hbm, v_hbm, y_ref,
-    d_buf, u_buf, v_buf, x_ref, acc_ref, wt_ref, c_ref, r_ref, total, got,
+    ranks_ref, b_ref, d_hbm, u_hbm, v_hbm, c_ref, moved_ref,
+    d_buf, v_buf, x_ref, acc_ref, wt_ref, r_ref, total, got,
     d_sem, u_sem, v_sem, send_sem, got_sem,
 ):
     me = lax.axis_index("leaf")
     rows = d_buf.shape[0]
     chunks = rows // chunk
-    state = u_buf.shape[1]
+    state = v_buf.shape[0]
     count = b_ref.shape[0]
     tiles = total.shape[0]
     bits = [lax.rem(lax.div(me, 1 << l), 2) for l in range(levels)]
@@ -45,7 +49,7 @@
         at = pl.ds(pl.multiple_of(m * chunk, chunk), chunk)
         return pltpu.make_async_copy(d_hbm.at[at, :], d_buf.at[at, :], d_sem.at[m])
 
-    u_copy = pltpu.make_async_copy(u_hbm, u_buf, u_sem)
+    u_copy = pltpu.make_async_copy(u_hbm, x_ref.at[pl.ds(0, state), :], u_sem)
     v_copy = pltpu.make_async_copy(v_hbm, v_buf, v_sem)
     u_copy.start()
     d_copy(0).start()
@@ -71,36 +75,25 @@
                 device_id_type=pl.DeviceIdType.MESH,
             )
 
-    edge = state // LANES * LANES
-    above = state - edge
     b = b_ref[...].astype(F32)
-    pieces = [b, jnp.zeros((LANES - above - count, rows), F32)]
-    if above:
-        pieces = [jnp.zeros((above, rows), F32)] + pieces
-    x_ref[:, edge:edge + LANES] = jnp.concatenate(pieces, axis=0).T.astype(BF16)
+    x_ref[state:state + 2 * count, :] = jnp.concatenate([b, b], axis=0).astype(BF16)
     u_copy.wait()
-    if edge:
-        x_ref[:, 0:edge] = u_buf[:, 0:edge]
-    if above:
-        x_ref[:, edge:state] = u_buf[:, edge:state]
     r_ref[...] = jnp.zeros_like(r_ref)
 
     def multiply(m):
         at = pl.ds(pl.multiple_of(m * chunk, chunk), chunk)
-        return dot(d_buf[at, :], x_ref[...])
+        return dot_turned(x_ref[...], d_buf[at, :])
 
     def project(m, block):
         at = pl.ds(pl.multiple_of(m * chunk, chunk), chunk)
-        turned = block.T
-        w = turned[0:state].astype(BF16)
-        c = turned[state:state + count]
-        c_ref[:, at] = c
-        high = c.astype(BF16).astype(F32)
-        both = jnp.concatenate([high, c - high], axis=0).astype(BF16)
+        w = block[0:state].astype(BF16)
+        twice = block[state:state + 2 * count]
+        c_ref[:, at] = twice[0:count]
+        high = twice.astype(BF16).astype(F32)
+        row = lax.broadcasted_iota(jnp.int32, twice.shape, 0)
+        both = jnp.where(row < count, high, twice - high).astype(BF16)
         wt_ref[:, at] = w
-        v = v_buf[at, :]
-        r_ref[0:state, :] += dot(w, v)
-        r_ref[state:state + 2 * count, :] += dot(both, v)
+        r_ref[...] += dot_turned(jnp.concatenate([w, both], axis=0), v_buf[:, at])
 
     d_copy(0).wait()
     acc_ref[0] = multiply(0)
@@ -260,7 +253,7 @@
     high = p.astype(BF16).astype(F32)
     both = jnp.concatenate([high, p - high], axis=0).astype(BF16)
     moved = dot(both, wt_ref[...])
-    y_ref[...] = c_ref[...] - (moved[0:count] + moved[count:2 * count])
+    moved_ref[...] = moved[0:count] + moved[count:2 * count]
 
     for l in range(levels):
         @pl.when(jnp.logical_and(is_last(l), bits[l] == 0))
@@ -276,26 +269,23 @@
     state = left_factors.shape[1]
     rank_top = state // levels
     tiles = pl.cdiv(state, LANES)
-    wide = pl.cdiv(state + count, LANES) * LANES
     chunk = rows // 8
     most = 0
     for l in range(levels):
         most = max(most, ((1 << l) - 1 + tiles) * (levels - l))
     vmem = pl.BlockSpec(memory_space=pltpu.VMEM)
     hbm = pl.BlockSpec(memory_space=pl.ANY)
-    return pl.pallas_call(
+    base, moved = pl.pallas_call(
         functools.partial(kernel, levels, rank_top, chunk),
-        out_shape=jax.ShapeDtypeStruct((count, rows), F32),
+        out_shape=[jax.ShapeDtypeStruct((count, rows), F32)] * 2,
         in_specs=[pl.BlockSpec(memory_space=pltpu.SMEM), vmem, hbm, hbm, hbm],
-        out_specs=vmem,
+        out_specs=[vmem, vmem],
         scratch_shapes=[
             pltpu.VMEM(diag_inverse.shape, BF16),
-            pltpu.VMEM((rows, state), BF16),
-            pltpu.VMEM((rows, state), BF16),
-            pltpu.VMEM((rows, wide), BF16),
-            pltpu.VMEM((2, chunk, wide), F32),
             pltpu.VMEM((state, rows), BF16),
-            pltpu.VMEM((count, rows), F32),
+            pltpu.VMEM((state + 2 * count, rows), BF16),
+            pltpu.VMEM((2, state + 2 * count, chunk), F32),
+            pltpu.VMEM((state, rows), BF16),
             pltpu.VMEM((state + 2 * count, state), F32),
             pltpu.VMEM((tiles, count + tiles * LANES, LANES), F32),
             pltpu.VMEM((levels, tiles, count + tiles * LANES, LANES), F32),
@@ -309,9 +299,10 @@
             collective_id=0, has_side_effects=True, vmem_limit_bytes=56 * 1024 * 1024
         ),
         cost_estimate=pl.CostEstimate(
-            flops=2 * rows * rows * wide, bytes_accessed=2 * rows * (rows + 2 * state), transcendentals=0
+            flops=2 * rows * rows * (state + count), bytes_accessed=2 * rows * (rows + 2 * state), transcendentals=0
         ),
-    )(ranks, rhs_vectors, diag_inverse, left_factors, right_factors)
+    )(ranks, rhs_vectors, diag_inverse, left_factors.T, right_factors.T)
+    return base - moved
 
 
 def solution(mesh):

time: 23.7 us -> 19.5 us (0.82)
  local copies, waits for them, and re-layouts: 5.94 us -> 0 us
  other arithmetic: 0 us -> 1.51 us
  Pallas kernels: 17.5 us -> 17.8 us
    unnamed x3 -> x0, local copies, waits for them, and re-layouts: 5.94 us -> none
    sub x0 -> x1, other arithmetic: none -> 1.51 us  [on_device(): return base - moved]
    pallas_call x1, Pallas kernels: 17.5 us -> 17.8 us  [on_device(): pl.pallas_call(functools.partial(kernel, levels, rank_top, chunk), out_sh...]
where the time goes in v2:
time: 19.5 us; the launch traced here: 19.3 us
  Pallas kernels  17.8 us (91%)
  other arithmetic  1.51 us (8%)
    pallas_call x1, Pallas kernels, on_device(): pl.pallas_call(functools.partial(kernel, levels, rank_top, chunk), out_sh...  17.8 us
    sub x1, other arithmetic, on_device(): return base - moved  1.51 us

profile of v2, /device:TPU:20, one launch (start us, length us, event | category | flops | bytes accessed | tf_op | source)
XLA Modules:
  0.0 19.3 jit_solution(2537769220749852991)
XLA Ops:
  0.0 17.8 %shard_map.55 = (f32[8,2048]{1,0:T(8,128)}, f32[8,2048]{1,0:T(8,128)}) custom-call(s32[3]{0:T(128)} %ranks_ref.1, bf16[8,2048]{1,0:T(8,128)(2,1)} %b_ref.1, bf16[2048,2048]{1,0:T(8,128)(2,1)} %d_hbm.1, bf16[192,2048]{1,0:T(8,128)(2,1)} %bitcast.2, bf16[192,2048]{1,0:T(8,128)(2,1)} %bitcast.3), custom_call_target="tpu_custom_call" | custom-call | flops 1677721600 | bytes 9961472 | tf_op jit(solution)/shard_map/pallas_call | solution.py:278
  17.8 1.5 %sub.3 = f32[8,2048]{1,0:T(8,128)} subtract(f32[8,2048]{1,0:T(8,128)} %get-tuple-element.7, f32[8,2048]{1,0:T(8,128)} %get-tuple-element.8) | non-fusion elementwise | flops 16384 | bytes 196608 | tf_op jit(solution)/shard_map/sub | solution.py:305

commit v3 on v2

--- a/solution.py
+++ b/solution.py
@@ -34,7 +34,7 @@
 def kernel(
     levels, rank_top, chunk,
     ranks_ref, b_ref, d_hbm, u_hbm, v_hbm, c_ref, moved_ref,
-    d_buf, v_buf, x_ref, acc_ref, wt_ref, r_ref, total, got,
+    d_buf, v_buf, x_ref, wt_ref, r_ref, total, got,
     d_sem, u_sem, v_sem, send_sem, got_sem,
 ):
     me = lax.axis_index("leaf")
@@ -46,7 +46,7 @@
     bits = [lax.rem(lax.div(me, 1 << l), 2) for l in range(levels)]
 
     def d_copy(m):
-        at = pl.ds(pl.multiple_of(m * chunk, chunk), chunk)
+        at = pl.ds(m * chunk, chunk)
         return pltpu.make_async_copy(d_hbm.at[at, :], d_buf.at[at, :], d_sem.at[m])
 
     u_copy = pltpu.make_async_copy(u_hbm, x_ref.at[pl.ds(0, state), :], u_sem)
@@ -81,11 +81,11 @@
     r_ref[...] = jnp.zeros_like(r_ref)
 
     def multiply(m):
-        at = pl.ds(pl.multiple_of(m * chunk, chunk), chunk)
+        at = pl.ds(m * chunk, chunk)
         return dot_turned(x_ref[...], d_buf[at, :])
 
     def project(m, block):
-        at = pl.ds(pl.multiple_of(m * chunk, chunk), chunk)
+        at = pl.ds(m * chunk, chunk)
         w = block[0:state].astype(BF16)
         twice = block[state:state + 2 * count]
         c_ref[:, at] = twice[0:count]
@@ -95,20 +95,16 @@
         wt_ref[:, at] = w
         r_ref[...] += dot_turned(jnp.concatenate([w, both], axis=0), v_buf[:, at])
 
-    d_copy(0).wait()
-    acc_ref[0] = multiply(0)
-    v_copy.wait()
-
-    def body(m, carry):
+    block = None
+    for m in range(chunks):
         d_copy(m).wait()
-        before = acc_ref[lax.rem(m + 1, 2)]
-        block = multiply(m)
-        project(m - 1, before)
-        acc_ref[lax.rem(m, 2)] = block
-        return carry
-
-    lax.fori_loop(1, chunks, body, 0)
-    project(chunks - 1, acc_ref[(chunks - 1) % 2])
+        if m == 1:
+            v_copy.wait()
+        after = multiply(m)
+        if m:
+            project(m - 1, block)
+        block = after
+    project(chunks - 1, block)
 
     lane = lax.broadcasted_iota(jnp.int32, (1, state), 1)
     limit = jnp.zeros((1, state), jnp.int32)
@@ -269,12 +265,12 @@
     state = left_factors.shape[1]
     rank_top = state // levels
     tiles = pl.cdiv(state, LANES)
-    chunk = rows // 8
+    chunk = rows // 4
     most = 0
     for l in range(levels):
         most = max(most, ((1 << l) - 1 + tiles) * (levels - l))
     vmem = pl.BlockSpec(memory_space=pltpu.VMEM)
-    hbm = pl.BlockSpec(memory_space=pl.ANY)
+    hbm = pl.BlockSpec(memory_space=pltpu.HBM)
     base, moved = pl.pallas_call(
         functools.partial(kernel, levels, rank_top, chunk),
         out_shape=[jax.ShapeDtypeStruct((count, rows), F32)] * 2,
@@ -284,7 +280,6 @@
             pltpu.VMEM(diag_inverse.shape, BF16),
             pltpu.VMEM((state, rows), BF16),
             pltpu.VMEM((state + 2 * count, rows), BF16),
-            pltpu.VMEM((2, state + 2 * count, chunk), F32),
             pltpu.VMEM((state, rows), BF16),
             pltpu.VMEM((state + 2 * count, state), F32),
             pltpu.VMEM((tiles, count + tiles * LANES, LANES), F32),
@@ -296,7 +291,7 @@
             pltpu.SemaphoreType.DMA((levels, tiles, levels + 1)),
         ],
         compiler_params=pltpu.CompilerParams(
-            collective_id=0, has_side_effects=True, vmem_limit_bytes=56 * 1024 * 1024
+            collective_id=0, has_side_effects=True, vmem_limit_bytes=55040 * 1024
         ),
         cost_estimate=pl.CostEstimate(
             flops=2 * rows * rows * (state + count), bytes_accessed=2 * rows * (rows + 2 * state), transcendentals=0

time: 19.5 us -> 18 us (0.923)
  Pallas kernels: 17.8 us -> 15.7 us
  local copies, waits for them, and re-layouts: 0 us -> 1.41 us
  other arithmetic: 1.51 us -> 0.64 us
    pallas_call x1, Pallas kernels: 17.8 us -> 15.7 us  [on_device(): pl.pallas_call(functools.partial(kernel, levels, rank_top, chunk), out_sh...]
    unnamed x0 -> x4, local copies, waits for them, and re-layouts: none -> 1.41 us
    sub x1, other arithmetic: 1.51 us -> 0.64 us  [on_device(): return base - moved]
where the time goes in v3:
time: 18 us; the launch traced here: 17.8 us
  Pallas kernels  15.7 us (87%)
  local copies, waits for them, and re-layouts  1.41 us (8%)
  other arithmetic  0.64 us (4%)
    pallas_call x1, Pallas kernels, on_device(): pl.pallas_call(functools.partial(kernel, levels, rank_top, chunk), out_sh...  15.7 us
    unnamed x4, local copies, waits for them, and re-layouts  1.41 us
    sub x1, other arithmetic, on_device(): return base - moved  0.64 us

profile of v3, /device:TPU:20, one launch (start us, length us, event | category | flops | bytes accessed | tf_op | source)
XLA Modules:
  0.0 17.8 jit_solution(203584406604825820)
XLA Ops:
  0.0 0.0 copy-start
  0.0 0.8 %copy-done = bf16[8,2048]{1,0:T(8,128)(2,1)S(1)} copy-done((bf16[8,2048]{1,0:T(8,128)(2,1)S(1)}, bf16[8,2048]{1,0:T(8,128)(2,1)}, u32[]{:S(2)}) %copy-start) | copy-done | bytes 32792
  0.8 0.0 copy-start.1
  0.8 0.7 %copy-done.1 = s32[3]{0:T(128)S(1)} copy-done((s32[3]{0:T(128)S(1)}, s32[3]{0:T(128)}, u32[]{:S(2)}) %copy-start.1) | copy-done | bytes 36
  1.4 15.7 %shard_map.55 = (f32[8,2048]{1,0:T(8,128)S(1)}, f32[8,2048]{1,0:T(8,128)S(1)}) custom-call(s32[3]{0:T(128)S(1)} %copy-done.1, bf16[8,2048]{1,0:T(8,128)(2,1)S(1)} %copy-done, bf16[2048,2048]{1,0:T(8,128)(2,1)} %d_hbm.1, bf16[192,2048]{1,0:T(8,128)(2,1)} %bitcast.2, bf16[192,2048]{1,0:T(8,128)(2,1)} %bitcast.3), custom_call_target="tpu_custom_call" | custom-call | flops 1677721600 | bytes 9961472 | tf_op jit(solution)/shard_map/pallas_call | solution.py:274
  17.2 0.6 %sub.3 = f32[8,2048]{1,0:T(8,128)} subtract(f32[8,2048]{1,0:T(8,128)S(1)} %get-tuple-element.7, f32[8,2048]{1,0:T(8,128)S(1)} %get-tuple-element.8) | non-fusion elementwise | flops 16384 | bytes 196608 | tf_op jit(solution)/shard_map/sub | solution.py:300
Async XLA Ops:
  0.0 0.8 %copy-start = (bf16[8,2048]{1,0:T(8,128)(2,1)S(1)}, bf16[8,2048]{1,0:T(8,128)(2,1)}, u32[]{:S(2)}) copy-start(bf16[8,2048]{1,0:T(8,128)(2,1)} %b_ref.1) | copy-start | bytes 98308
  0.8 0.7 %copy-start.1 = (s32[3]{0:T(128)S(1)}, s32[3]{0:T(128)}, u32[]{:S(2)}) copy-start(s32[3]{0:T(128)} %ranks_ref.1) | copy-start | bytes 40

commit v4 on v3

--- a/solution.py
+++ b/solution.py
@@ -21,10 +21,6 @@
     return jnp.dot(a, b, preferred_element_type=F32)
 
 
-def dot_turned(a, b):
-    return lax.dot_general(a, b, (((1,), (1,)), ((), ())), preferred_element_type=F32)
-
-
 def dot_split(a, b):
     a_high, a_low = split(a)
     b_high, b_low = split(b)
@@ -34,7 +30,7 @@
 def kernel(
     levels, rank_top, chunk,
     ranks_ref, b_ref, d_hbm, u_hbm, v_hbm, c_ref, moved_ref,
-    d_buf, v_buf, x_ref, wt_ref, r_ref, total, got,
+    d_buf, v_buf, turned_ref, x_ref, w_ref, tall_ref, wt_ref, total, got,
     d_sem, u_sem, v_sem, send_sem, got_sem,
 ):
     me = lax.axis_index("leaf")
@@ -49,7 +45,7 @@
         at = pl.ds(m * chunk, chunk)
         return pltpu.make_async_copy(d_hbm.at[at, :], d_buf.at[at, :], d_sem.at[m])
 
-    u_copy = pltpu.make_async_copy(u_hbm, x_ref.at[pl.ds(0, state), :], u_sem)
+    u_copy = pltpu.make_async_copy(u_hbm, turned_ref.at[pl.ds(0, state), :], u_sem)
     v_copy = pltpu.make_async_copy(v_hbm, v_buf, v_sem)
     u_copy.start()
     d_copy(0).start()
@@ -75,42 +71,45 @@
                 device_id_type=pl.DeviceIdType.MESH,
             )
 
+    wide = x_ref.shape[1]
     b = b_ref[...].astype(F32)
-    x_ref[state:state + 2 * count, :] = jnp.concatenate([b, b], axis=0).astype(BF16)
+    pad = jnp.zeros((wide - state - 2 * count, rows), F32)
+    turned_ref[state:wide, :] = jnp.concatenate([b, b, pad], axis=0).astype(BF16)
     u_copy.wait()
-    r_ref[...] = jnp.zeros_like(r_ref)
+    x_ref[...] = turned_ref[...].T
+
+    edge = state // LANES * LANES
+    above = state - edge
+    low = lax.broadcasted_iota(jnp.int32, (1, wide), 1) >= state + count
 
     def multiply(m):
-        at = pl.ds(m * chunk, chunk)
-        return dot_turned(x_ref[...], d_buf[at, :])
+        return dot(d_buf[m * chunk:(m + 1) * chunk, :], x_ref[...])
 
     def project(m, block):
-        at = pl.ds(m * chunk, chunk)
-        w = block[0:state].astype(BF16)
-        twice = block[state:state + 2 * count]
-        c_ref[:, at] = twice[0:count]
-        high = twice.astype(BF16).astype(F32)
-        row = lax.broadcasted_iota(jnp.int32, twice.shape, 0)
-        both = jnp.where(row < count, high, twice - high).astype(BF16)
-        wt_ref[:, at] = w
-        r_ref[...] += dot_turned(jnp.concatenate([w, both], axis=0), v_buf[:, at])
+        at = slice(m * chunk, (m + 1) * chunk)
+        tall_ref[at, :] = block[:, edge:edge + LANES]
+        high = block.astype(BF16)
+        both = jnp.where(low, block - high.astype(F32), block).astype(BF16)
+        w_ref[at, :] = both
+        return dot(v_buf[:, at], both)
 
     block = None
+    r = jnp.zeros((state, wide), F32)
     for m in range(chunks):
         d_copy(m).wait()
         if m == 1:
             v_copy.wait()
         after = multiply(m)
         if m:
-            project(m - 1, block)
+            r = r + project(m - 1, block)
         block = after
-    project(chunks - 1, block)
+    r = (r + project(chunks - 1, block)).T
 
     lane = lax.broadcasted_iota(jnp.int32, (1, state), 1)
     limit = jnp.zeros((1, state), jnp.int32)
     for l in range(levels):
         limit = jnp.where(lane // rank_top == l, ranks_ref[l], limit)
-    r = jnp.where(lane % rank_top < limit, r_ref[...], 0.0)
+    r = jnp.where(lane % rank_top < limit, r, 0.0)
     for t in range(tiles):
         wide = min(LANES, state - t * LANES)
         part = r[:, t * LANES:t * LANES + wide]
@@ -207,6 +206,26 @@
             def _():
                 update(count + (l + 1) * rank_top, count + state)
 
+    def absorb(l):
+        own = tile_of(l)
+        start = l * rank_top - own * LANES
+        row = lax.broadcasted_iota(jnp.int32, (LANES, LANES), 0)
+        inside = jnp.logical_and(row >= start, row < start + rank_top)
+
+        def update(lo, hi):
+            factor = got[l, own, lo:hi, :]
+            for c in range(l):
+                t = tile_of(c)
+                at = count + own * LANES
+                step = jnp.where(inside, got[c, t, at:at + LANES, :], 0.0)
+                got[c, t, lo:hi, :] = got[c, t, lo:hi, :] + dot_split(factor, step)
+
+        update(0, count)
+        if l + 1 < levels:
+            @pl.when(lax.div(me, 2 << l) > 0)
+            def _():
+                update(count + (l + 1) * rank_top, count + state)
+
     for l in range(levels):
         sends = jnp.logical_and(is_last(l), bits[l] == 0)
         if l:
@@ -221,30 +240,31 @@
             for _, condition, copy in copies(l):
                 guarded(condition, copy.start)
 
+        if l == levels - 1:
+            c_ref[...] = tall_ref[...].T[above:above + count]
+            wt_ref[...] = w_ref[:, 0:state].T
+
         @pl.when(takes)
         def _():
             receive(l)
             if l + 1 < levels:
                 join(l)
+            if l:
+                absorb(l)
 
         if others is not None:
             @pl.when(others)
             def _():
                 receive_narrow(l)
-
-    wide = tiles * LANES
+                absorb(l)
+
     lane = lax.broadcasted_iota(jnp.int32, (1, LANES), 1)
     parts = [jnp.zeros((count, LANES), F32)] * tiles
-    for l in range(levels - 1, -1, -1):
+    for l in range(levels):
         t = tile_of(l)
-        value = got[l, t, 0:count, :]
-        if l + 1 < levels:
-            value = value + dot_split(
-                jnp.concatenate(parts, axis=1), got[l, t, count:count + wide, :]
-            )
         start = l * rank_top - t * LANES
         inside = jnp.logical_and(lane >= start, lane < start + rank_top)
-        parts[t] = jnp.where(inside, value, parts[t])
+        parts[t] = jnp.where(inside, got[l, t, 0:count, :], parts[t])
     p = jnp.concatenate(parts, axis=1)[:, 0:state]
     high = p.astype(BF16).astype(F32)
     both = jnp.concatenate([high, p - high], axis=0).astype(BF16)
@@ -266,6 +286,7 @@
     rank_top = state // levels
     tiles = pl.cdiv(state, LANES)
     chunk = rows // 4
+    wide = pl.cdiv(state + 2 * count, LANES) * LANES
     most = 0
     for l in range(levels):
         most = max(most, ((1 << l) - 1 + tiles) * (levels - l))
@@ -279,9 +300,11 @@
         scratch_shapes=[
             pltpu.VMEM(diag_inverse.shape, BF16),
             pltpu.VMEM((state, rows), BF16),
-            pltpu.VMEM((state + 2 * count, rows), BF16),
+            pltpu.VMEM((wide, rows), BF16),
+            pltpu.VMEM((rows, wide), BF16),
+            pltpu.VMEM((rows, wide), BF16),
+            pltpu.VMEM((rows, LANES), F32),
             pltpu.VMEM((state, rows), BF16),
-            pltpu.VMEM((state + 2 * count, state), F32),
             pltpu.VMEM((tiles, count + tiles * LANES, LANES), F32),
             pltpu.VMEM((levels, tiles, count + tiles * LANES, LANES), F32),
             pltpu.SemaphoreType.DMA((rows // chunk,)),
@@ -294,7 +317,7 @@
             collective_id=0, has_side_effects=True, vmem_limit_bytes=55040 * 1024
         ),
         cost_estimate=pl.CostEstimate(
-            flops=2 * rows * rows * (state + count), bytes_accessed=2 * rows * (rows + 2 * state), transcendentals=0
+            flops=2 * rows * rows * wide, bytes_accessed=2 * rows * (rows + 2 * state), transcendentals=0
         ),
     )(ranks, rhs_vectors, diag_inverse, left_factors.T, right_factors.T)
     return base - moved

time: 18 us -> 19.7 us (1.094)
  Pallas kernels: 15.7 us -> 17.4 us
    pallas_call x1, Pallas kernels: 15.7 us -> 17.4 us  [on_device(): pl.pallas_call(functools.partial(kernel, levels, rank_top, chunk), out_sh...]
where the time goes in v4:
time: 19.7 us; the launch traced here: 19.5 us
  Pallas kernels  17.4 us (88%)
  local copies, waits for them, and re-layouts  1.41 us (7%)
  other arithmetic  0.64 us (3%)
    pallas_call x1, Pallas kernels, on_device(): pl.pallas_call(functools.partial(kernel, levels, rank_top, chunk), out_sh...  17.4 us
    unnamed x4, local copies, waits for them, and re-layouts  1.41 us
    sub x1, other arithmetic, on_device(): return base - moved  0.64 us

profile of v4, /device:TPU:20, one launch (start us, length us, event | category | flops | bytes accessed | tf_op | source)
XLA Modules:
  0.0 19.5 jit_solution(935159956028755170)
XLA Ops:
  0.0 0.0 copy-start
  0.0 0.8 %copy-done = bf16[8,2048]{1,0:T(8,128)(2,1)S(1)} copy-done((bf16[8,2048]{1,0:T(8,128)(2,1)S(1)}, bf16[8,2048]{1,0:T(8,128)(2,1)}, u32[]{:S(2)}) %copy-start) | copy-done | bytes 32792
  0.8 0.0 copy-start.1
  0.8 0.7 %copy-done.1 = s32[3]{0:T(128)S(1)} copy-done((s32[3]{0:T(128)S(1)}, s32[3]{0:T(128)}, u32[]{:S(2)}) %copy-start.1) | copy-done | bytes 36
  1.4 17.4 %shard_map.55 = (f32[8,2048]{1,0:T(8,128)S(1)}, f32[8,2048]{1,0:T(8,128)S(1)}) custom-call(s32[3]{0:T(128)S(1)} %copy-done.1, bf16[8,2048]{1,0:T(8,128)(2,1)S(1)} %copy-done, bf16[2048,2048]{1,0:T(8,128)(2,1)} %d_hbm.1, bf16[192,2048]{1,0:T(8,128)(2,1)} %bitcast.2, bf16[192,2048]{1,0:T(8,128)(2,1)} %bitcast.3), custom_call_target="tpu_custom_call" | custom-call | flops 2147483648 | bytes 9961472 | tf_op jit(solution)/shard_map/pallas_call | solution.py:295
  18.9 0.6 %sub.3 = f32[8,2048]{1,0:T(8,128)} subtract(f32[8,2048]{1,0:T(8,128)S(1)} %get-tuple-element.7, f32[8,2048]{1,0:T(8,128)S(1)} %get-tuple-element.8) | non-fusion elementwise | flops 16384 | bytes 196608 | tf_op jit(solution)/shard_map/sub | solution.py:323
Async XLA Ops:
  0.0 0.8 %copy-start = (bf16[8,2048]{1,0:T(8,128)(2,1)S(1)}, bf16[8,2048]{1,0:T(8,128)(2,1)}, u32[]{:S(2)}) copy-start(bf16[8,2048]{1,0:T(8,128)(2,1)} %b_ref.1) | copy-start | bytes 98308
  0.8 0.7 %copy-start.1 = (s32[3]{0:T(128)S(1)}, s32[3]{0:T(128)}, u32[]{:S(2)}) copy-start(s32[3]{0:T(128)} %ranks_ref.1) | copy-start | bytes 40

commit v5 on v3

--- a/solution.py
+++ b/solution.py
@@ -45,17 +45,18 @@
     tiles = total.shape[0]
     bits = [lax.rem(lax.div(me, 1 << l), 2) for l in range(levels)]
 
+    pieces = d_sem.shape[0]
+    piece = rows // pieces
+    flight = 3
+
     def d_copy(m):
-        at = pl.ds(m * chunk, chunk)
+        at = pl.ds(m * piece, piece)
         return pltpu.make_async_copy(d_hbm.at[at, :], d_buf.at[at, :], d_sem.at[m])
 
     u_copy = pltpu.make_async_copy(u_hbm, x_ref.at[pl.ds(0, state), :], u_sem)
     v_copy = pltpu.make_async_copy(v_hbm, v_buf, v_sem)
     u_copy.start()
     d_copy(0).start()
-    v_copy.start()
-    for m in range(1, chunks):
-        d_copy(m).start()
 
     def sender_of(l):
         span = 2 << l
@@ -78,6 +79,8 @@
     b = b_ref[...].astype(F32)
     x_ref[state:state + 2 * count, :] = jnp.concatenate([b, b], axis=0).astype(BF16)
     u_copy.wait()
+    for m in range(1, flight):
+        d_copy(m).start()
     r_ref[...] = jnp.zeros_like(r_ref)
 
     def multiply(m):
@@ -96,8 +99,14 @@
         r_ref[...] += dot_turned(jnp.concatenate([w, both], axis=0), v_buf[:, at])
 
     block = None
+    per = chunk // piece
     for m in range(chunks):
-        d_copy(m).wait()
+        for part in range(m * per, (m + 1) * per):
+            d_copy(part).wait()
+            if part + flight < pieces:
+                d_copy(part + flight).start()
+            if part == 0:
+                v_copy.start()
         if m == 1:
             v_copy.wait()
         after = multiply(m)
@@ -207,6 +216,26 @@
             def _():
                 update(count + (l + 1) * rank_top, count + state)
 
+    def absorb(l):
+        own = tile_of(l)
+        start = l * rank_top - own * LANES
+        row = lax.broadcasted_iota(jnp.int32, (LANES, LANES), 0)
+        inside = jnp.logical_and(row >= start, row < start + rank_top)
+
+        def update(lo, hi):
+            factor = got[l, own, lo:hi, :]
+            for c in range(l):
+                t = tile_of(c)
+                at = count + own * LANES
+                step = jnp.where(inside, got[c, t, at:at + LANES, :], 0.0)
+                got[c, t, lo:hi, :] = got[c, t, lo:hi, :] + dot_split(factor, step)
+
+        update(0, count)
+        if l + 1 < levels:
+            @pl.when(lax.div(me, 2 << l) > 0)
+            def _():
+                update(count + (l + 1) * rank_top, count + state)
+
     for l in range(levels):
         sends = jnp.logical_and(is_last(l), bits[l] == 0)
         if l:
@@ -226,25 +255,22 @@
             receive(l)
             if l + 1 < levels:
                 join(l)
+            if l:
+                absorb(l)
 
         if others is not None:
             @pl.when(others)
             def _():
                 receive_narrow(l)
-
-    wide = tiles * LANES
+                absorb(l)
+
     lane = lax.broadcasted_iota(jnp.int32, (1, LANES), 1)
     parts = [jnp.zeros((count, LANES), F32)] * tiles
-    for l in range(levels - 1, -1, -1):
+    for l in range(levels):
         t = tile_of(l)
-        value = got[l, t, 0:count, :]
-        if l + 1 < levels:
-            value = value + dot_split(
-                jnp.concatenate(parts, axis=1), got[l, t, count:count + wide, :]
-            )
         start = l * rank_top - t * LANES
         inside = jnp.logical_and(lane >= start, lane < start + rank_top)
-        parts[t] = jnp.where(inside, value, parts[t])
+        parts[t] = jnp.where(inside, got[l, t, 0:count, :], parts[t])
     p = jnp.concatenate(parts, axis=1)[:, 0:state]
     high = p.astype(BF16).astype(F32)
     both = jnp.concatenate([high, p - high], axis=0).astype(BF16)
@@ -284,7 +310,7 @@
             pltpu.VMEM((state + 2 * count, state), F32),
             pltpu.VMEM((tiles, count + tiles * LANES, LANES), F32),
             pltpu.VMEM((levels, tiles, count + tiles * LANES, LANES), F32),
-            pltpu.SemaphoreType.DMA((rows // chunk,)),
+            pltpu.SemaphoreType.DMA((8,)),
             pltpu.SemaphoreType.DMA,
             pltpu.SemaphoreType.DMA,
             pltpu.SemaphoreType.DMA((most,)),

time: 18 us -> 18 us (level)
  no operation moved by 1% of the time
where the time goes in v5:
time: 18 us; the launch traced here: 17.8 us
  Pallas kernels  15.7 us (87%)
  local copies, waits for them, and re-layouts  1.41 us (8%)
  other arithmetic  0.64 us (4%)
    pallas_call x1, Pallas kernels, on_device(): pl.pallas_call(functools.partial(kernel, levels, rank_top, chunk), out_sh...  15.7 us
    unnamed x4, local copies, waits for them, and re-layouts  1.41 us
    sub x1, other arithmetic, on_device(): return base - moved  0.64 us

profile of v5, /device:TPU:20, one launch (start us, length us, event | category | flops | bytes accessed | tf_op | source)
XLA Modules:
  0.0 17.8 jit_solution(11190052838403048117)
XLA Ops:
  0.0 0.0 copy-start
  0.0 0.8 %copy-done = bf16[8,2048]{1,0:T(8,128)(2,1)S(1)} copy-done((bf16[8,2048]{1,0:T(8,128)(2,1)S(1)}, bf16[8,2048]{1,0:T(8,128)(2,1)}, u32[]{:S(2)}) %copy-start) | copy-done | bytes 32792
  0.8 0.0 copy-start.1
  0.8 0.7 %copy-done.1 = s32[3]{0:T(128)S(1)} copy-done((s32[3]{0:T(128)S(1)}, s32[3]{0:T(128)}, u32[]{:S(2)}) %copy-start.1) | copy-done | bytes 36
  1.4 15.7 %shard_map.55 = (f32[8,2048]{1,0:T(8,128)S(1)}, f32[8,2048]{1,0:T(8,128)S(1)}) custom-call(s32[3]{0:T(128)S(1)} %copy-done.1, bf16[8,2048]{1,0:T(8,128)(2,1)S(1)} %copy-done, bf16[2048,2048]{1,0:T(8,128)(2,1)} %d_hbm.1, bf16[192,2048]{1,0:T(8,128)(2,1)} %bitcast.2, bf16[192,2048]{1,0:T(8,128)(2,1)} %bitcast.3), custom_call_target="tpu_custom_call" | custom-call | flops 1677721600 | bytes 9961472 | tf_op jit(solution)/shard_map/pallas_call | solution.py:300
  17.1 0.6 %sub.3 = f32[8,2048]{1,0:T(8,128)} subtract(f32[8,2048]{1,0:T(8,128)S(1)} %get-tuple-element.7, f32[8,2048]{1,0:T(8,128)S(1)} %get-tuple-element.8) | non-fusion elementwise | flops 16384 | bytes 196608 | tf_op jit(solution)/shard_map/sub | solution.py:326
Async XLA Ops:
  0.0 0.8 %copy-start = (bf16[8,2048]{1,0:T(8,128)(2,1)S(1)}, bf16[8,2048]{1,0:T(8,128)(2,1)}, u32[]{:S(2)}) copy-start(bf16[8,2048]{1,0:T(8,128)(2,1)} %b_ref.1) | copy-start | bytes 98308
  0.8 0.7 %copy-start.1 = (s32[3]{0:T(128)S(1)}, s32[3]{0:T(128)}, u32[]{:S(2)}) copy-start(s32[3]{0:T(128)} %ranks_ref.1) | copy-start | bytes 40

commit v6 on v5

--- a/solution.py
+++ b/solution.py
@@ -56,7 +56,8 @@
     u_copy = pltpu.make_async_copy(u_hbm, x_ref.at[pl.ds(0, state), :], u_sem)
     v_copy = pltpu.make_async_copy(v_hbm, v_buf, v_sem)
     u_copy.start()
-    d_copy(0).start()
+    for m in range(flight):
+        d_copy(m).start()
 
     def sender_of(l):
         span = 2 << l
@@ -79,8 +80,6 @@
     b = b_ref[...].astype(F32)
     x_ref[state:state + 2 * count, :] = jnp.concatenate([b, b], axis=0).astype(BF16)
     u_copy.wait()
-    for m in range(1, flight):
-        d_copy(m).start()
     r_ref[...] = jnp.zeros_like(r_ref)
 
     def multiply(m):
@@ -250,19 +249,21 @@
             for _, condition, copy in copies(l):
                 guarded(condition, copy.start)
 
+        if l > 1:
+            pl.when(bits[l - 1] == 1)(functools.partial(absorb, l - 1))
+
         @pl.when(takes)
         def _():
             receive(l)
             if l + 1 < levels:
                 join(l)
-            if l:
-                absorb(l)
 
         if others is not None:
             @pl.when(others)
             def _():
                 receive_narrow(l)
-                absorb(l)
+
+    pl.when(bits[levels - 1] == 1)(functools.partial(absorb, levels - 1))
 
     lane = lax.broadcasted_iota(jnp.int32, (1, LANES), 1)
     parts = [jnp.zeros((count, LANES), F32)] * tiles

time: 18 us -> 17.8 us (0.989)
  Pallas kernels: 15.7 us -> 15.5 us
    pallas_call x1, Pallas kernels: 15.7 us -> 15.5 us  [on_device(): pl.pallas_call(functools.partial(kernel, levels, rank_top, chunk), out_sh...]
where the time goes in v6:
time: 17.8 us; the launch traced here: 17.5 us
  Pallas kernels  15.5 us (87%)
  local copies, waits for them, and re-layouts  1.41 us (8%)
  other arithmetic  0.64 us (4%)
    pallas_call x1, Pallas kernels, on_device(): pl.pallas_call(functools.partial(kernel, levels, rank_top, chunk), out_sh...  15.5 us
    unnamed x4, local copies, waits for them, and re-layouts  1.41 us
    sub x1, other arithmetic, on_device(): return base - moved  0.64 us

profile of v6, /device:TPU:20, one launch (start us, length us, event | category | flops | bytes accessed | tf_op | source)
XLA Modules:
  0.0 17.5 jit_solution(2822934794343711851)
XLA Ops:
  0.0 0.0 copy-start
  0.0 0.8 %copy-done = bf16[8,2048]{1,0:T(8,128)(2,1)S(1)} copy-done((bf16[8,2048]{1,0:T(8,128)(2,1)S(1)}, bf16[8,2048]{1,0:T(8,128)(2,1)}, u32[]{:S(2)}) %copy-start) | copy-done | bytes 32792
  0.8 0.0 copy-start.1
  0.8 0.7 %copy-done.1 = s32[3]{0:T(128)S(1)} copy-done((s32[3]{0:T(128)S(1)}, s32[3]{0:T(128)}, u32[]{:S(2)}) %copy-start.1) | copy-done | bytes 36
  1.4 15.5 %shard_map.55 = (f32[8,2048]{1,0:T(8,128)S(1)}, f32[8,2048]{1,0:T(8,128)S(1)}) custom-call(s32[3]{0:T(128)S(1)} %copy-done.1, bf16[8,2048]{1,0:T(8,128)(2,1)S(1)} %copy-done, bf16[2048,2048]{1,0:T(8,128)(2,1)} %d_hbm.1, bf16[192,2048]{1,0:T(8,128)(2,1)} %bitcast.2, bf16[192,2048]{1,0:T(8,128)(2,1)} %bitcast.3), custom_call_target="tpu_custom_call" | custom-call | flops 1677721600 | bytes 9961472 | tf_op jit(solution)/shard_map/pallas_call | solution.py:301
  16.9 0.6 %sub.3 = f32[8,2048]{1,0:T(8,128)} subtract(f32[8,2048]{1,0:T(8,128)S(1)} %get-tuple-element.7, f32[8,2048]{1,0:T(8,128)S(1)} %get-tuple-element.8) | non-fusion elementwise | flops 16384 | bytes 196608 | tf_op jit(solution)/shard_map/sub | solution.py:327
Async XLA Ops:
  0.0 0.8 %copy-start = (bf16[8,2048]{1,0:T(8,128)(2,1)S(1)}, bf16[8,2048]{1,0:T(8,128)(2,1)}, u32[]{:S(2)}) copy-start(bf16[8,2048]{1,0:T(8,128)(2,1)} %b_ref.1) | copy-start | bytes 98308
  0.8 0.7 %copy-start.1 = (s32[3]{0:T(128)S(1)}, s32[3]{0:T(128)}, u32[]{:S(2)}) copy-start(s32[3]{0:T(128)} %ranks_ref.1) | copy-start | bytes 40

commit v7 on v6

--- a/solution.py
+++ b/solution.py
@@ -26,20 +26,21 @@
 
 
 def dot_split(a, b):
-    a_high, a_low = split(a)
-    b_high, b_low = split(b)
-    return dot(a_high, b_high) + (dot(a_high, b_low) + dot(a_low, b_high))
+    n = a.shape[0]
+    high = a.astype(BF16).astype(F32)
+    both = jnp.concatenate([high, a - high], axis=0).astype(BF16)
+    whole = dot(both, b[0]) + dot(both, b[1])
+    return whole[0:n] + whole[n:2 * n]
 
 
 def kernel(
-    levels, rank_top, chunk,
+    levels, rank_top,
     ranks_ref, b_ref, d_hbm, u_hbm, v_hbm, c_ref, moved_ref,
     d_buf, v_buf, x_ref, wt_ref, r_ref, total, got,
     d_sem, u_sem, v_sem, send_sem, got_sem,
 ):
     me = lax.axis_index("leaf")
     rows = d_buf.shape[0]
-    chunks = rows // chunk
     state = v_buf.shape[0]
     count = b_ref.shape[0]
     tiles = total.shape[0]
@@ -82,12 +83,10 @@
     u_copy.wait()
     r_ref[...] = jnp.zeros_like(r_ref)
 
-    def multiply(m):
-        at = pl.ds(m * chunk, chunk)
+    def multiply(at):
         return dot_turned(x_ref[...], d_buf[at, :])
 
-    def project(m, block):
-        at = pl.ds(m * chunk, chunk)
+    def project(at, block):
         w = block[0:state].astype(BF16)
         twice = block[state:state + 2 * count]
         c_ref[:, at] = twice[0:count]
@@ -97,22 +96,22 @@
         wt_ref[:, at] = w
         r_ref[...] += dot_turned(jnp.concatenate([w, both], axis=0), v_buf[:, at])
 
-    block = None
-    per = chunk // piece
-    for m in range(chunks):
-        for part in range(m * per, (m + 1) * per):
+    block, before = None, None
+    for first, last in ((0, 2), (2, 4), (4, 6), (6, 7), (7, 8)):
+        for part in range(first, last):
             d_copy(part).wait()
             if part + flight < pieces:
                 d_copy(part + flight).start()
             if part == 0:
                 v_copy.start()
-        if m == 1:
+        if first == 2:
             v_copy.wait()
-        after = multiply(m)
-        if m:
-            project(m - 1, block)
-        block = after
-    project(chunks - 1, block)
+        at = pl.ds(first * piece, (last - first) * piece)
+        after = multiply(at)
+        if before is not None:
+            project(before, block)
+        block, before = after, at
+    project(before, block)
 
     lane = lax.broadcasted_iota(jnp.int32, (1, state), 1)
     limit = jnp.zeros((1, state), jnp.int32)
@@ -192,48 +191,45 @@
             )
             guarded([] if m is None else [bits[m] == 1], copy.wait_recv)
 
-    def join(l):
+    def level_rows(l, sources):
         own = tile_of(l)
         start = l * rank_top - own * LANES
         row = lax.broadcasted_iota(jnp.int32, (LANES, LANES), 0)
         inside = jnp.logical_and(row >= start, row < start + rank_top)
-
-        def update(lo, hi):
-            factor = got[l, own, lo:hi, :]
-            for t in range(tiles):
-                if all(tile_of(c) != t for c in range(l + 1, levels)):
-                    continue
-                at = count + own * LANES
-                step = jnp.where(inside, total[t, at:at + LANES, :], 0.0)
-                total[t, lo:hi, :] = (
-                    total[t, lo:hi, :] + got[l, t, lo:hi, :] + dot_split(factor, step)
-                )
-
-        update(0, count)
+        at = slice(count + own * LANES, count + (own + 1) * LANES)
+        parts = [jnp.where(inside, ref[at, :], 0.0) for ref in sources]
+        return split(jnp.concatenate(parts, axis=1))
+
+    def for_rows(l, update):
+        update(slice(0, count))
         if l + 1 < levels:
             @pl.when(lax.div(me, 2 << l) > 0)
             def _():
-                update(count + (l + 1) * rank_top, count + state)
-
-    def absorb(l):
-        own = tile_of(l)
-        start = l * rank_top - own * LANES
-        row = lax.broadcasted_iota(jnp.int32, (LANES, LANES), 0)
-        inside = jnp.logical_and(row >= start, row < start + rank_top)
-
-        def update(lo, hi):
-            factor = got[l, own, lo:hi, :]
+                update(slice(count + (l + 1) * rank_top, count + state))
+
+    def tiles_above(l):
+        return sorted({tile_of(c) for c in range(l + 1, levels)})
+
+    def join(l, factors):
+        def update(at):
+            step = dot_split(got[l, tile_of(l), at, :], factors)
+            for place, t in enumerate(tiles_above(l)):
+                mine = step[:, place * LANES:(place + 1) * LANES]
+                total[t, at, :] = total[t, at, :] + got[l, t, at, :] + mine
+
+        for_rows(l, update)
+
+    def absorb(l, factors):
+        def update(at):
+            step = dot_split(got[l, tile_of(l), at, :], factors)
             for c in range(l):
                 t = tile_of(c)
-                at = count + own * LANES
-                step = jnp.where(inside, got[c, t, at:at + LANES, :], 0.0)
-                got[c, t, lo:hi, :] = got[c, t, lo:hi, :] + dot_split(factor, step)
-
-        update(0, count)
-        if l + 1 < levels:
-            @pl.when(lax.div(me, 2 << l) > 0)
-            def _():
-                update(count + (l + 1) * rank_top, count + state)
+                got[c, t, at, :] = got[c, t, at, :] + step[:, c * LANES:(c + 1) * LANES]
+
+        for_rows(l, update)
+
+    def below(l):
+        return level_rows(l, [got.at[c, tile_of(c)] for c in range(l)])
 
     for l in range(levels):
         sends = jnp.logical_and(is_last(l), bits[l] == 0)
@@ -250,20 +246,30 @@
                 guarded(condition, copy.start)
 
         if l > 1:
-            pl.when(bits[l - 1] == 1)(functools.partial(absorb, l - 1))
+            @pl.when(bits[l - 1] == 1)
+            def _():
+                absorb(l - 1, below(l - 1))
+
+        if l == levels - 1:
+            @pl.when(bits[l] == 1)
+            def _():
+                factors = below(l) if l else None
+                receive_narrow(l)
+                if l:
+                    absorb(l, factors)
+
+            continue
 
         @pl.when(takes)
         def _():
+            factors = level_rows(l, [total.at[t] for t in tiles_above(l)])
             receive(l)
-            if l + 1 < levels:
-                join(l)
+            join(l, factors)
 
         if others is not None:
             @pl.when(others)
             def _():
                 receive_narrow(l)
-
-    pl.when(bits[levels - 1] == 1)(functools.partial(absorb, levels - 1))
 
     lane = lax.broadcasted_iota(jnp.int32, (1, LANES), 1)
     parts = [jnp.zeros((count, LANES), F32)] * tiles
@@ -292,14 +298,13 @@
     state = left_factors.shape[1]
     rank_top = state // levels
     tiles = pl.cdiv(state, LANES)
-    chunk = rows // 4
     most = 0
     for l in range(levels):
         most = max(most, ((1 << l) - 1 + tiles) * (levels - l))
     vmem = pl.BlockSpec(memory_space=pltpu.VMEM)
     hbm = pl.BlockSpec(memory_space=pltpu.HBM)
     base, moved = pl.pallas_call(
-        functools.partial(kernel, levels, rank_top, chunk),
+        functools.partial(kernel, levels, rank_top),
         out_shape=[jax.ShapeDtypeStruct((count, rows), F32)] * 2,
         in_specs=[pl.BlockSpec(memory_space=pltpu.SMEM), vmem, hbm, hbm, hbm],
         out_specs=[vmem, vmem],

time: 17.8 us -> 17.9 us (level)
  no operation moved by 1% of the time
where the time goes in v7:
time: 17.9 us; the launch traced here: 17.7 us
  Pallas kernels  15.6 us (87%)
  local copies, waits for them, and re-layouts  1.41 us (8%)
  other arithmetic  0.64 us (4%)
    pallas_call x1, Pallas kernels, on_device(): pl.pallas_call(functools.partial(kernel, levels, rank_top), out_shape=[ja...  15.6 us
    unnamed x4, local copies, waits for them, and re-layouts  1.41 us
    sub x1, other arithmetic, on_device(): return base - moved  0.64 us

profile of v7, /device:TPU:20, one launch (start us, length us, event | category | flops | bytes accessed | tf_op | source)
XLA Modules:
  0.0 17.7 jit_solution(14469323227459412834)
XLA Ops:
  0.0 0.0 copy-start
  0.0 0.8 %copy-done = bf16[8,2048]{1,0:T(8,128)(2,1)S(1)} copy-done((bf16[8,2048]{1,0:T(8,128)(2,1)S(1)}, bf16[8,2048]{1,0:T(8,128)(2,1)}, u32[]{:S(2)}) %copy-start) | copy-done | bytes 32792
  0.8 0.0 copy-start.1
  0.8 0.7 %copy-done.1 = s32[3]{0:T(128)S(1)} copy-done((s32[3]{0:T(128)S(1)}, s32[3]{0:T(128)}, u32[]{:S(2)}) %copy-start.1) | copy-done | bytes 36
  1.4 15.6 %shard_map.55 = (f32[8,2048]{1,0:T(8,128)S(1)}, f32[8,2048]{1,0:T(8,128)S(1)}) custom-call(s32[3]{0:T(128)S(1)} %copy-done.1, bf16[8,2048]{1,0:T(8,128)(2,1)S(1)} %copy-done, bf16[2048,2048]{1,0:T(8,128)(2,1)} %d_hbm.1, bf16[192,2048]{1,0:T(8,128)(2,1)} %bitcast.2, bf16[192,2048]{1,0:T(8,128)(2,1)} %bitcast.3), custom_call_target="tpu_custom_call" | custom-call | flops 1677721600 | bytes 9961472 | tf_op jit(solution)/shard_map/pallas_call | solution.py:306
  17.0 0.6 %sub.3 = f32[8,2048]{1,0:T(8,128)} subtract(f32[8,2048]{1,0:T(8,128)S(1)} %get-tuple-element.7, f32[8,2048]{1,0:T(8,128)S(1)} %get-tuple-element.8) | non-fusion elementwise | flops 16384 | bytes 196608 | tf_op jit(solution)/shard_map/sub | solution.py:332
Async XLA Ops:
  0.0 0.8 %copy-start = (bf16[8,2048]{1,0:T(8,128)(2,1)S(1)}, bf16[8,2048]{1,0:T(8,128)(2,1)}, u32[]{:S(2)}) copy-start(bf16[8,2048]{1,0:T(8,128)(2,1)} %b_ref.1) | copy-start | bytes 98308
  0.8 0.7 %copy-start.1 = (s32[3]{0:T(128)S(1)}, s32[3]{0:T(128)}, u32[]{:S(2)}) copy-start(s32[3]{0:T(128)} %ranks_ref.1) | copy-start | bytes 40

commit v8 on v7

--- a/solution.py
+++ b/solution.py
@@ -35,30 +35,14 @@
 
 def kernel(
     levels, rank_top,
-    ranks_ref, b_ref, d_hbm, u_hbm, v_hbm, c_ref, moved_ref,
-    d_buf, v_buf, x_ref, wt_ref, r_ref, total, got,
-    d_sem, u_sem, v_sem, send_sem, got_sem,
+    ranks_ref, block_ref, v_ref, c_ref, moved_ref,
+    wt_ref, total, got, send_sem, got_sem,
 ):
     me = lax.axis_index("leaf")
-    rows = d_buf.shape[0]
-    state = v_buf.shape[0]
-    count = b_ref.shape[0]
+    state, rows = v_ref.shape
+    count = c_ref.shape[0]
     tiles = total.shape[0]
     bits = [lax.rem(lax.div(me, 1 << l), 2) for l in range(levels)]
-
-    pieces = d_sem.shape[0]
-    piece = rows // pieces
-    flight = 3
-
-    def d_copy(m):
-        at = pl.ds(m * piece, piece)
-        return pltpu.make_async_copy(d_hbm.at[at, :], d_buf.at[at, :], d_sem.at[m])
-
-    u_copy = pltpu.make_async_copy(u_hbm, x_ref.at[pl.ds(0, state), :], u_sem)
-    v_copy = pltpu.make_async_copy(v_hbm, v_buf, v_sem)
-    u_copy.start()
-    for m in range(flight):
-        d_copy(m).start()
 
     def sender_of(l):
         span = 2 << l
@@ -78,46 +62,20 @@
                 device_id_type=pl.DeviceIdType.MESH,
             )
 
-    b = b_ref[...].astype(F32)
-    x_ref[state:state + 2 * count, :] = jnp.concatenate([b, b], axis=0).astype(BF16)
-    u_copy.wait()
-    r_ref[...] = jnp.zeros_like(r_ref)
-
-    def multiply(at):
-        return dot_turned(x_ref[...], d_buf[at, :])
-
-    def project(at, block):
-        w = block[0:state].astype(BF16)
-        twice = block[state:state + 2 * count]
-        c_ref[:, at] = twice[0:count]
-        high = twice.astype(BF16).astype(F32)
-        row = lax.broadcasted_iota(jnp.int32, twice.shape, 0)
-        both = jnp.where(row < count, high, twice - high).astype(BF16)
-        wt_ref[:, at] = w
-        r_ref[...] += dot_turned(jnp.concatenate([w, both], axis=0), v_buf[:, at])
-
-    block, before = None, None
-    for first, last in ((0, 2), (2, 4), (4, 6), (6, 7), (7, 8)):
-        for part in range(first, last):
-            d_copy(part).wait()
-            if part + flight < pieces:
-                d_copy(part + flight).start()
-            if part == 0:
-                v_copy.start()
-        if first == 2:
-            v_copy.wait()
-        at = pl.ds(first * piece, (last - first) * piece)
-        after = multiply(at)
-        if before is not None:
-            project(before, block)
-        block, before = after, at
-    project(before, block)
+    w = block_ref[0:state, :].astype(BF16)
+    wt_ref[...] = w
+    twice = block_ref[state:state + 2 * count, :]
+    c_ref[...] = twice[0:count]
+    high = twice.astype(BF16).astype(F32)
+    row = lax.broadcasted_iota(jnp.int32, twice.shape, 0)
+    both = jnp.where(row < count, high, twice - high).astype(BF16)
+    r = dot_turned(jnp.concatenate([w, both], axis=0), v_ref[...])
 
     lane = lax.broadcasted_iota(jnp.int32, (1, state), 1)
     limit = jnp.zeros((1, state), jnp.int32)
     for l in range(levels):
         limit = jnp.where(lane // rank_top == l, ranks_ref[l], limit)
-    r = jnp.where(lane % rank_top < limit, r_ref[...], 0.0)
+    r = jnp.where(lane % rank_top < limit, r, 0.0)
     for t in range(tiles):
         wide = min(LANES, state - t * LANES)
         part = r[:, t * LANES:t * LANES + wide]
@@ -302,33 +260,31 @@
     for l in range(levels):
         most = max(most, ((1 << l) - 1 + tiles) * (levels - l))
     vmem = pl.BlockSpec(memory_space=pltpu.VMEM)
-    hbm = pl.BlockSpec(memory_space=pltpu.HBM)
+    joined = jnp.concatenate([left_factors.T, rhs_vectors, rhs_vectors], axis=0)
+    mapped = lax.dot_general(
+        joined, diag_inverse, (((1,), (1,)), ((), ())), preferred_element_type=F32
+    )
     base, moved = pl.pallas_call(
         functools.partial(kernel, levels, rank_top),
         out_shape=[jax.ShapeDtypeStruct((count, rows), F32)] * 2,
-        in_specs=[pl.BlockSpec(memory_space=pltpu.SMEM), vmem, hbm, hbm, hbm],
+        in_specs=[pl.BlockSpec(memory_space=pltpu.SMEM), vmem, vmem],
         out_specs=[vmem, vmem],
         scratch_shapes=[
-            pltpu.VMEM(diag_inverse.shape, BF16),
             pltpu.VMEM((state, rows), BF16),
-            pltpu.VMEM((state + 2 * count, rows), BF16),
-            pltpu.VMEM((state, rows), BF16),
-            pltpu.VMEM((state + 2 * count, state), F32),
             pltpu.VMEM((tiles, count + tiles * LANES, LANES), F32),
             pltpu.VMEM((levels, tiles, count + tiles * LANES, LANES), F32),
-            pltpu.SemaphoreType.DMA((8,)),
-            pltpu.SemaphoreType.DMA,
-            pltpu.SemaphoreType.DMA,
             pltpu.SemaphoreType.DMA((most,)),
             pltpu.SemaphoreType.DMA((levels, tiles, levels + 1)),
         ],
         compiler_params=pltpu.CompilerParams(
-            collective_id=0, has_side_effects=True, vmem_limit_bytes=55040 * 1024
+            collective_id=0, has_side_effects=True, vmem_limit_bytes=50 * 1024 * 1024
         ),
         cost_estimate=pl.CostEstimate(
-            flops=2 * rows * rows * (state + count), bytes_accessed=2 * rows * (rows + 2 * state), transcendentals=0
+            flops=2 * rows * state * (state + 2 * count),
+            bytes_accessed=6 * rows * state,
+            transcendentals=0,
         ),
-    )(ranks, rhs_vectors, diag_inverse, left_factors.T, right_factors.T)
+    )(ranks, mapped, right_factors.T)
     return base - moved
 
 

time: 17.9 us -> 17.7 us (0.989)
  matrix products: 0 us -> 6.53 us
  Pallas kernels: 15.6 us -> 10.3 us
  local copies, waits for them, and re-layouts: 1.41 us -> 0.01 us
    dot_general x0 -> x1, matrix products: none -> 6.53 us  [on_device(): lax.dot_general(joined, diag_inverse, (((1,), (1,)), ((), ())), preferred...]
    pallas_call x1, Pallas kernels: 15.6 us -> 10.3 us  [on_device(): pl.pallas_call(functools.partial(kernel, levels, rank_top), out_shape=[ja...]
    unnamed x4, local copies, waits for them, and re-layouts: 1.41 us -> 0.01 us
where the time goes in v8:
time: 17.7 us; the launch traced here: 17.5 us
  Pallas kernels  10.3 us (58%)
  matrix products  6.53 us (37%)
  other arithmetic  0.64 us (4%)
    pallas_call x1, Pallas kernels, on_device(): pl.pallas_call(functools.partial(kernel, levels, rank_top), out_shape=[ja...  10.3 us
    dot_general x1, matrix products, on_device(): lax.dot_general(joined, diag_inverse, (((1,), (1,)), ((), ())), preferred...  6.53 us
    sub x1, other arithmetic, on_device(): return base - moved  0.64 us

profile of v8, /device:TPU:20, one launch (start us, length us, event | category | flops | bytes accessed | tf_op | source)
XLA Modules:
  0.0 17.5 jit_solution(15144916385979306209)
XLA Ops:
  0.0 0.0 copy-start
  0.0 0.0 copy-start.1
  0.0 6.5 %fusion.block_ref = f32[208,2048]{1,0:T(8,128)S(1)} fusion(bf16[2048,2048]{1,0:T(8,128)(2,1)} %param.6, bf16[8,2048]{1,0:T(8,128)(2,1)} %param.5, bf16[192,2048]{1,0:T(8,128)(2,1)} %bitcast.4), kind=kOutput, calls=%fused_computation | convolution fusion | flops 1747386368 | bytes 10911744 | tf_op jit(solution)/shard_map/dot_general | solution.py:264
  6.5 0.0 copy-done
  6.6 0.0 copy-done.1
  6.6 10.3 %shard_map.55 = (f32[8,2048]{1,0:T(8,128)S(1)}, f32[8,2048]{1,0:T(8,128)S(1)}) custom-call(s32[3]{0:T(128)S(1)} %copy-done.1, f32[208,2048]{1,0:T(8,128)S(1)} %fusion.block_ref, bf16[192,2048]{1,0:T(8,128)(2,1)S(1)} %bitcast.3), custom_call_target="tpu_custom_call" | custom-call | flops 163577856 | bytes 2359296 | tf_op jit(solution)/shard_map/pallas_call | solution.py:267
  16.9 0.6 %sub.3 = f32[8,2048]{1,0:T(8,128)} subtract(f32[8,2048]{1,0:T(8,128)S(1)} %get-tuple-element.7, f32[8,2048]{1,0:T(8,128)S(1)} %get-tuple-element.8) | non-fusion elementwise | flops 16384 | bytes 196608 | tf_op jit(solution)/shard_map/sub | solution.py:288
Async XLA Ops:
  0.0 6.5 %copy-start = (bf16[2048,192]{0,1:T(8,128)(2,1)S(1)}, bf16[2048,192]{0,1:T(8,128)(2,1)}, u32[]{:S(2)}) copy-start(bf16[2048,192]{0,1:T(8,128)(2,1)} %param.8) | copy-start | bytes 2359300
  0.0 6.6 %copy-start.1 = (s32[3]{0:T(128)S(1)}, s32[3]{0:T(128)}, u32[]{:S(2)}) copy-start(s32[3]{0:T(128)} %ranks_ref.1) | copy-start | bytes 40

commit v9 on v6

--- a/solution.py
+++ b/solution.py
@@ -33,7 +33,7 @@
 
 def kernel(
     levels, rank_top, chunk,
-    ranks_ref, b_ref, d_hbm, u_hbm, v_hbm, c_ref, moved_ref,
+    ranks_ref, b_ref, block_ref, d_hbm, u_hbm, v_hbm, c_ref, moved_ref,
     d_buf, v_buf, x_ref, wt_ref, r_ref, total, got,
     d_sem, u_sem, v_sem, send_sem, got_sem,
 ):
@@ -48,6 +48,7 @@
     pieces = d_sem.shape[0]
     piece = rows // pieces
     flight = 3
+    per = chunk // piece
 
     def d_copy(m):
         at = pl.ds(m * piece, piece)
@@ -56,8 +57,9 @@
     u_copy = pltpu.make_async_copy(u_hbm, x_ref.at[pl.ds(0, state), :], u_sem)
     v_copy = pltpu.make_async_copy(v_hbm, v_buf, v_sem)
     u_copy.start()
-    for m in range(flight):
+    for m in range(per, per + flight):
         d_copy(m).start()
+    v_copy.start()
 
     def sender_of(l):
         span = 2 << l
@@ -97,20 +99,16 @@
         wt_ref[:, at] = w
         r_ref[...] += dot_turned(jnp.concatenate([w, both], axis=0), v_buf[:, at])
 
-    block = None
-    per = chunk // piece
-    for m in range(chunks):
+    block = block_ref[...]
+    for m in range(1, chunks):
         for part in range(m * per, (m + 1) * per):
             d_copy(part).wait()
             if part + flight < pieces:
                 d_copy(part + flight).start()
-            if part == 0:
-                v_copy.start()
         if m == 1:
             v_copy.wait()
         after = multiply(m)
-        if m:
-            project(m - 1, block)
+        project(m - 1, block)
         block = after
     project(chunks - 1, block)
 
@@ -296,12 +294,16 @@
     most = 0
     for l in range(levels):
         most = max(most, ((1 << l) - 1 + tiles) * (levels - l))
+    joined = jnp.concatenate([left_factors.T, rhs_vectors, rhs_vectors], axis=0)
+    mapped = lax.dot_general(
+        joined, diag_inverse[:chunk], (((1,), (1,)), ((), ())), preferred_element_type=F32
+    )
     vmem = pl.BlockSpec(memory_space=pltpu.VMEM)
     hbm = pl.BlockSpec(memory_space=pltpu.HBM)
     base, moved = pl.pallas_call(
         functools.partial(kernel, levels, rank_top, chunk),
         out_shape=[jax.ShapeDtypeStruct((count, rows), F32)] * 2,
-        in_specs=[pl.BlockSpec(memory_space=pltpu.SMEM), vmem, hbm, hbm, hbm],
+        in_specs=[pl.BlockSpec(memory_space=pltpu.SMEM), vmem, vmem, hbm, hbm, hbm],
         out_specs=[vmem, vmem],
         scratch_shapes=[
             pltpu.VMEM(diag_inverse.shape, BF16),
@@ -318,12 +320,12 @@
             pltpu.SemaphoreType.DMA((levels, tiles, levels + 1)),
         ],
         compiler_params=pltpu.CompilerParams(
-            collective_id=0, has_side_effects=True, vmem_limit_bytes=55040 * 1024
+            collective_id=0, has_side_effects=True, vmem_limit_bytes=52 * 1024 * 1024
         ),
         cost_estimate=pl.CostEstimate(
             flops=2 * rows * rows * (state + count), bytes_accessed=2 * rows * (rows + 2 * state), transcendentals=0
         ),
-    )(ranks, rhs_vectors, diag_inverse, left_factors.T, right_factors.T)
+    )(ranks, rhs_vectors, mapped, diag_inverse, left_factors.T, right_factors.T)
     return base - moved
 
 

time: 17.8 us -> 17.9 us (level)
  matrix products: 0 us -> 2.78 us
  local copies, waits for them, and re-layouts: 1.41 us -> 0.01 us
  Pallas kernels: 15.5 us -> 14.3 us
    dot_general x0 -> x1, matrix products: none -> 2.78 us  [on_device(): lax.dot_general(joined, diag_inverse[:chunk], (((1,), (1,)), ((), ())), p...]
    unnamed x4 -> x6, local copies, waits for them, and re-layouts: 1.41 us -> 0.01 us
    pallas_call x1, Pallas kernels: 15.5 us -> 14.3 us  [on_device(): pl.pallas_call(functools.partial(kernel, levels, rank_top, chunk), out_sh...]
where the time goes in v9:
time: 17.9 us; the launch traced here: 17.7 us
  Pallas kernels  14.3 us (80%)
  matrix products  2.78 us (16%)
  other arithmetic  0.64 us (4%)
    pallas_call x1, Pallas kernels, on_device(): pl.pallas_call(functools.partial(kernel, levels, rank_top, chunk), out_sh...  14.3 us
    dot_general x1, matrix products, on_device(): lax.dot_general(joined, diag_inverse[:chunk], (((1,), (1,)), ((), ())), p...  2.78 us
    sub x1, other arithmetic, on_device(): return base - moved  0.64 us

profile of v9, /device:TPU:20, one launch (start us, length us, event | category | flops | bytes accessed | tf_op | source)
XLA Modules:
  0.0 17.7 jit_solution(1936282244475831162)
XLA Ops:
  0.0 0.0 copy-start
  0.0 0.0 copy-start.1
  0.0 0.0 copy-start.2
  0.0 2.8 %fusion.block_ref = f32[208,512]{1,0:T(8,128)S(1)} fusion(bf16[2048,2048]{1,0:T(8,128)(2,1)} %d_hbm.1, bf16[8,2048]{1,0:T(8,128)(2,1)} %b_ref.1, bf16[192,2048]{1,0:T(8,128)(2,1)} %bitcast.2), kind=kOutput, calls=%fused_computation | convolution fusion | flops 438763520 | bytes 3342336 | tf_op jit(solution)/shard_map/dot_general | solution.py:298
  2.8 0.0 copy-done
  2.8 0.0 copy-done.1
  2.8 0.0 copy-done.2
  2.8 14.3 %shard_map.55 = (f32[8,2048]{1,0:T(8,128)S(1)}, f32[8,2048]{1,0:T(8,128)S(1)}) custom-call(s32[3]{0:T(128)S(1)} %copy-done.2, bf16[8,2048]{1,0:T(8,128)(2,1)S(1)} %copy-done.1, f32[208,512]{1,0:T(8,128)S(1)} %fusion.block_ref, bf16[2048,2048]{1,0:T(8,128)(2,1)} %d_hbm.1, bf16[192,2048]{1,0:T(8,128)(2,1)S(1)} %bitcast.3, bf16[192,2048]{1,0:T(8,128)(2,1)} %bitcast.4), custom_call_target="tpu_custom_call" | custom-call | flops 1677721600 | bytes 9961472 | tf_op jit(solution)/shard_map/pallas_call | solution.py:303
  17.1 0.6 %sub.3 = f32[8,2048]{1,0:T(8,128)} subtract(f32[8,2048]{1,0:T(8,128)S(1)} %get-tuple-element.7, f32[8,2048]{1,0:T(8,128)S(1)} %get-tuple-element.8) | non-fusion elementwise | flops 16384 | bytes 196608 | tf_op jit(solution)/shard_map/sub | solution.py:329
Async XLA Ops:
  0.0 2.8 %copy-start = (bf16[2048,192]{0,1:T(8,128)(2,1)S(1)}, bf16[2048,192]{0,1:T(8,128)(2,1)}, u32[]{:S(2)}) copy-start(bf16[2048,192]{0,1:T(8,128)(2,1)} %param.7) | copy-start | bytes 2359300
  0.0 2.8 %copy-start.1 = (bf16[8,2048]{1,0:T(8,128)(2,1)S(1)}, bf16[8,2048]{1,0:T(8,128)(2,1)}, u32[]{:S(2)}) copy-start(bf16[8,2048]{1,0:T(8,128)(2,1)} %b_ref.1) | copy-start | bytes 98308
  0.0 2.8 %copy-start.2 = (s32[3]{0:T(128)S(1)}, s32[3]{0:T(128)}, u32[]{:S(2)}) copy-start(s32[3]{0:T(128)} %ranks_ref.1) | copy-start | bytes 40

commit v10 on v8

--- a/solution.py
+++ b/solution.py
@@ -35,12 +35,12 @@
 
 def kernel(
     levels, rank_top,
-    ranks_ref, block_ref, v_ref, c_ref, moved_ref,
+    ranks_ref, block_ref, v_ref, moved_ref,
     wt_ref, total, got, send_sem, got_sem,
 ):
     me = lax.axis_index("leaf")
     state, rows = v_ref.shape
-    count = c_ref.shape[0]
+    count = moved_ref.shape[0]
     tiles = total.shape[0]
     bits = [lax.rem(lax.div(me, 1 << l), 2) for l in range(levels)]
 
@@ -65,7 +65,6 @@
     w = block_ref[0:state, :].astype(BF16)
     wt_ref[...] = w
     twice = block_ref[state:state + 2 * count, :]
-    c_ref[...] = twice[0:count]
     high = twice.astype(BF16).astype(F32)
     row = lax.broadcasted_iota(jnp.int32, twice.shape, 0)
     both = jnp.where(row < count, high, twice - high).astype(BF16)
@@ -264,11 +263,11 @@
     mapped = lax.dot_general(
         joined, diag_inverse, (((1,), (1,)), ((), ())), preferred_element_type=F32
     )
-    base, moved = pl.pallas_call(
+    moved = pl.pallas_call(
         functools.partial(kernel, levels, rank_top),
-        out_shape=[jax.ShapeDtypeStruct((count, rows), F32)] * 2,
+        out_shape=jax.ShapeDtypeStruct((count, rows), F32),
         in_specs=[pl.BlockSpec(memory_space=pltpu.SMEM), vmem, vmem],
-        out_specs=[vmem, vmem],
+        out_specs=vmem,
         scratch_shapes=[
             pltpu.VMEM((state, rows), BF16),
             pltpu.VMEM((tiles, count + tiles * LANES, LANES), F32),
@@ -285,7 +284,7 @@
             transcendentals=0,
         ),
     )(ranks, mapped, right_factors.T)
-    return base - moved
+    return mapped[state:state + count] - moved
 
 
 def solution(mesh):

time: 17.7 us -> 17.7 us (level)
  no operation moved by 1% of the time
where the time goes in v10:
time: 17.7 us; the launch traced here: 17.5 us
  Pallas kernels  10.3 us (58%)
  matrix products  6.53 us (37%)
  other arithmetic  0.64 us (4%)
    pallas_call x1, Pallas kernels, on_device(): pl.pallas_call(functools.partial(kernel, levels, rank_top), out_shape=jax...  10.3 us
    dot_general x1, matrix products, on_device(): lax.dot_general(joined, diag_inverse, (((1,), (1,)), ((), ())), preferred...  6.53 us
    sub x1, other arithmetic, on_device(): return mapped[state:state + count] - moved  0.64 us

profile of v10, /device:TPU:20, one launch (start us, length us, event | category | flops | bytes accessed | tf_op | source)
XLA Modules:
  0.0 17.5 jit_solution(2750227664108001446)
XLA Ops:
  0.0 0.0 copy-start
  0.0 0.0 copy-start.1
  0.0 6.5 %fusion.block_ref = f32[208,2048]{1,0:T(8,128)S(1)} fusion(bf16[2048,2048]{1,0:T(8,128)(2,1)} %param.6, bf16[8,2048]{1,0:T(8,128)(2,1)} %param.5, bf16[192,2048]{1,0:T(8,128)(2,1)} %bitcast.4), kind=kOutput, calls=%fused_computation | convolution fusion | flops 1747386368 | bytes 10911744 | tf_op jit(solution)/shard_map/dot_general | solution.py:263
  6.5 0.0 copy-done
  6.6 0.0 copy-done.1
  6.6 10.3 %shard_map.55 = f32[8,2048]{1,0:T(8,128)S(1)} custom-call(s32[3]{0:T(128)S(1)} %copy-done.1, f32[208,2048]{1,0:T(8,128)S(1)} %fusion.block_ref, bf16[192,2048]{1,0:T(8,128)(2,1)S(1)} %bitcast.3), custom_call_target="tpu_custom_call" | custom-call | flops 163577856 | bytes 2359296 | tf_op jit(solution)/shard_map/pallas_call | solution.py:266
  16.9 0.6 %slice_subtract_fusion = f32[8,2048]{1,0:T(8,128)} fusion(f32[8,2048]{1,0:T(8,128)S(1)} %shard_map.55, f32[208,2048]{1,0:T(8,128)S(1)} %fusion.block_ref), kind=kLoop, calls=%fused_computation.6 | loop fusion | flops 16384 | bytes 196608 | tf_op jit(solution)/shard_map/sub | solution.py:287
Async XLA Ops:
  0.0 6.5 %copy-start = (bf16[2048,192]{0,1:T(8,128)(2,1)S(1)}, bf16[2048,192]{0,1:T(8,128)(2,1)}, u32[]{:S(2)}) copy-start(bf16[2048,192]{0,1:T(8,128)(2,1)} %param.8) | copy-start | bytes 2359300
  0.0 6.6 %copy-start.1 = (s32[3]{0:T(128)S(1)}, s32[3]{0:T(128)}, u32[]{:S(2)}) copy-start(s32[3]{0:T(128)} %ranks_ref.1) | copy-start | bytes 40
